TPU v7x, 128 devices: a whole 4x4x4 slice. The times are simulated.
128 devices in a mesh: pair: 32 (over z, x, core), atom: 4 (over y).
Axes of the slice: x: 4, y: 4, z: 4, core: 2. Of those that a mesh axis runs over, the one named last changes fastest.
Arguments:
- pair_state: bfloat16 [512, 512, 128], P('pair', 'atom'), may hold values from -6 to 6
- cotangent: bfloat16 [512, 512, 128], P('pair', 'atom'), may hold values from -6 to 6
- atom_feats: bfloat16 [16384, 128], P(('pair', 'atom')), may hold values from -6 to 6
- atom_token: int32 [16384], P(('pair', 'atom')), may hold values from 0 to 511, as said below
- window_count: int32 [512], P(('pair', 'atom')), may hold values from 24 to 32, as said below
- input_weight: bfloat16 [128, 640], replicated, may hold values from -0.5 to 0.5
- output_weight: bfloat16 [128, 128], replicated, may hold values from -0.5 to 0.5
- atom_weight: bfloat16 [128, 384], replicated, may hold values from -0.5 to 0.5
- left_weight: bfloat16 [384, 128], replicated, may hold values from -0.3125 to 0.3125
- right_weight: bfloat16 [384, 128], replicated, may hold values from -0.3125 to 0.3125
Outputs:
- pair_grad: bfloat16 [512, 512, 128], P('pair', 'atom')
- atom_grad: bfloat16 [16384, 128], P(('pair', 'atom'))
Inputs may be any that keep to these rules, and one draw needn't show every extreme that they name: `atom_token`: taken in slot order, the live slots' tokens never fall, and every token from 0 to 511 is the token of at least one live slot. The device at position d of pair+atom holds slots d * 128 to (d + 1) * 128 - 1; its live slots belong to tokens d * 4 to (d + 1) * 4 - 1, except on every device but the first a leading run of one to four live slots that belong to token d * 4 - 1. A dead slot carries the token of the live slot before it. `window_count`: window 0 is full and window 1 holds exactly 24 live slots in every draw.
All inputs are finite; a program needn't handle non-finite values.
Results may differ from a plain program's by a relative error of at most 0.015.
Values may be sent and summed in bfloat16 or wider, within the bound.
A program may use at most 64 MiB of HBM per device.

v0:
```python
import jax
import jax.numpy as jnp
from jax import lax
from jax.sharding import PartitionSpec as P

EPSILON = 1e-05
HIGHEST = lax.Precision.HIGHEST


def shifted_2(x, axis, by):
    length = lax.axis_size(axis)
    pairs = [(i, i + by) for i in range(length) if 0 <= i + by < length]
    return lax.ppermute(x, axis, pairs)


def layer_stats(values, axis):
    centre = jnp.mean(values, axis=axis, keepdims=True)
    shifted = values - centre
    inverse = lax.rsqrt(jnp.mean(shifted * shifted, axis=axis, keepdims=True) + EPSILON)
    return (shifted * inverse, inverse)


def layer_backward(upstream, normed, inverse, axis):
    first_mean = jnp.mean(upstream, axis=axis, keepdims=True)
    cross_mean = jnp.mean(upstream * normed, axis=axis, keepdims=True)
    return inverse * (upstream - first_mean - normed * cross_mean)


def to_channels(stacked):
    pair_count = lax.axis_size("pair")
    atom_count = lax.axis_size("atom")
    device_count = pair_count * atom_count
    stack_size, hidden, row_count, col_count = stacked.shape
    per_device = hidden // device_count
    shaped = stacked.reshape(stack_size, device_count, per_device, row_count, col_count)
    arrived = lax.all_to_all(shaped, ("pair", "atom"), split_axis=1, concat_axis=1, tiled=True)
    arrived = arrived.reshape(stack_size, pair_count, atom_count, per_device, row_count, col_count)
    arrived = arrived.transpose(0, 3, 1, 4, 2, 5)
    return arrived.reshape(stack_size, per_device, row_count * pair_count, col_count * atom_count)


def to_pairs(stacked):
    pair_count = lax.axis_size("pair")
    atom_count = lax.axis_size("atom")
    device_count = pair_count * atom_count
    stack_size, per_device, tokens, tokens_again = stacked.shape
    row_count = tokens // pair_count
    col_count = tokens_again // atom_count
    shaped = stacked.reshape(stack_size, per_device, pair_count, row_count, atom_count, col_count)
    shaped = shaped.transpose(0, 2, 4, 1, 3, 5).reshape(
        stack_size, device_count, per_device, row_count, col_count
    )
    arrived = lax.all_to_all(shaped, ("pair", "atom"), split_axis=1, concat_axis=1, tiled=True)
    return arrived.reshape(stack_size, device_count * per_device, row_count, col_count)


def body(
    pair_state,
    cotangent,
    atom_feats,
    atom_token,
    window_count,
    input_weight,
    output_weight,
    atom_weight,
    left_weight,
    right_weight,
):
    pair_count = lax.axis_size("pair")
    atom_count = lax.axis_size("atom")
    row_count, col_count, channels = pair_state.shape
    tokens = row_count * pair_count
    per_owner = tokens // (pair_count * atom_count)
    hidden = output_weight.shape[0]
    slot_total = atom_feats.shape[0]
    window_span = slot_total // window_count.shape[0]
    live_slot = jnp.arange(slot_total) % window_span < jnp.repeat(window_count, window_span)
    pair_index = lax.axis_index("pair")
    atom_index = lax.axis_index("atom")
    atom_pre = jnp.dot(atom_feats, atom_weight, preferred_element_type=jnp.float32)
    atom_hidden = jax.nn.silu(atom_pre).astype(jnp.bfloat16)
    member = ((atom_token[None, :] == jnp.arange(tokens)[:, None]) & live_slot[None, :]).astype(
        jnp.bfloat16
    )
    first_token = (pair_index * atom_count + atom_index) * per_owner
    own_member = (
        (atom_token[None, :] == first_token + jnp.arange(per_owner)[:, None]) & live_slot[None, :]
    ).astype(jnp.bfloat16)
    own_sums = jnp.dot(own_member, atom_hidden, preferred_element_type=jnp.float32)
    own_counts = jnp.sum(own_member.astype(jnp.float32), axis=1)
    lead_member = ((atom_token == first_token - 1) & live_slot).astype(jnp.bfloat16)
    lead_sum = jnp.dot(lead_member[None, :], atom_hidden, preferred_element_type=jnp.float32)
    lead_count = jnp.sum(lead_member.astype(jnp.float32), keepdims=True)
    came_sum, came_count = shifted_2((lead_sum, lead_count), ("pair", "atom"), -1)
    tail_mask = (jnp.arange(per_owner) == per_owner - 1).astype(jnp.float32)
    owner_sums = own_sums + tail_mask[:, None] * came_sum
    owner_counts = own_counts + tail_mask * came_count
    single = (owner_sums / owner_counts[:, None]).astype(jnp.bfloat16)
    left_own = jnp.dot(single, left_weight, preferred_element_type=jnp.float32).astype(jnp.bfloat16)
    right_own = jnp.dot(single, right_weight, preferred_element_type=jnp.float32).astype(
        jnp.bfloat16
    )
    biases, counts_all = (
        lax.all_gather(
            jnp.concatenate([left_own, right_own], axis=1), ("pair", "atom"), axis=0, tiled=True
        ),
        lax.all_gather(owner_counts.astype(jnp.bfloat16), ("pair", "atom"), axis=0, tiled=True),
    )
    left_rows = lax.dynamic_slice_in_dim(biases[:, :channels], pair_index * row_count, row_count, 0)
    right_cols = lax.dynamic_slice_in_dim(
        biases[:, channels:], atom_index * col_count, col_count, 0
    )
    inputs = (
        pair_state.astype(jnp.float32)
        + left_rows.astype(jnp.float32)[:, None, :]
        + right_cols.astype(jnp.float32)[None, :, :]
    )
    normed, inverse = layer_stats(inputs, 2)
    hidden_in = normed.astype(jnp.bfloat16)
    pieces = [
        jnp.einsum(
            "rkc,ch->hrk",
            hidden_in,
            input_weight[:, quarter * hidden : (quarter + 1) * hidden],
            preferred_element_type=jnp.float32,
        )
        for quarter in range(4)
    ]
    gate_pre = jnp.einsum(
        "rkc,cd->rkd", hidden_in, input_weight[:, 4 * hidden :], preferred_element_type=jnp.float32
    )
    left_edge = (jax.nn.sigmoid(pieces[1]) * pieces[0]).astype(jnp.bfloat16)
    right_edge = (jax.nn.sigmoid(pieces[3]) * pieces[2]).astype(jnp.bfloat16)
    channel_edges = to_channels(jnp.stack([left_edge, right_edge]))
    product = jnp.einsum(
        "cik,cjk->cij", channel_edges[0], channel_edges[1], preferred_element_type=jnp.float32
    ).astype(jnp.bfloat16)
    returned = to_pairs(product[None])[0]
    prod_normed, prod_inverse = layer_stats(returned.astype(jnp.float32), 0)
    update_pre = jnp.einsum(
        "hrk,hd->rkd",
        prod_normed.astype(jnp.bfloat16),
        output_weight,
        preferred_element_type=jnp.float32,
    )
    gate_open = jax.nn.sigmoid(gate_pre)
    incoming = cotangent.astype(jnp.float32)
    grad_gate = (incoming * update_pre * gate_open * (1.0 - gate_open)).astype(jnp.bfloat16)
    grad_update = (incoming * gate_open).astype(jnp.bfloat16)
    grad_normed = jnp.einsum(
        "rkd,hd->hrk", grad_update, output_weight, preferred_element_type=jnp.float32
    )
    grad_product = layer_backward(grad_normed, prod_normed, prod_inverse, 0).astype(jnp.bfloat16)
    grad_channel = to_channels(grad_product[None])[0]
    left_grad = jnp.einsum(
        "cij,cjk->cik", grad_channel, channel_edges[1], preferred_element_type=jnp.float32
    ).astype(jnp.bfloat16)
    right_grad = jnp.einsum(
        "cij,cik->cjk", grad_channel, channel_edges[0], preferred_element_type=jnp.float32
    ).astype(jnp.bfloat16)
    edge_grads = to_pairs(jnp.stack([left_grad, right_grad]))
    left_flow = edge_grads[0].astype(jnp.float32)
    right_flow = edge_grads[1].astype(jnp.float32)
    left_sigmoid = jax.nn.sigmoid(pieces[1])
    right_sigmoid = jax.nn.sigmoid(pieces[3])
    branch_grads = [
        (left_flow * left_sigmoid).astype(jnp.bfloat16),
        (left_flow * pieces[0] * left_sigmoid * (1.0 - left_sigmoid)).astype(jnp.bfloat16),
        (right_flow * right_sigmoid).astype(jnp.bfloat16),
        (right_flow * pieces[2] * right_sigmoid * (1.0 - right_sigmoid)).astype(jnp.bfloat16),
    ]
    grad_hidden = jnp.einsum(
        "rkd,cd->rkc", grad_gate, input_weight[:, 4 * hidden :], preferred_element_type=jnp.float32
    )
    for quarter in range(4):
        grad_hidden = grad_hidden + jnp.einsum(
            "hrk,ch->rkc",
            branch_grads[quarter],
            input_weight[:, quarter * hidden : (quarter + 1) * hidden],
            preferred_element_type=jnp.float32,
        )
    grad_inputs = layer_backward(grad_hidden, normed, inverse, 2)
    pair_grad = grad_inputs.astype(jnp.bfloat16)
    row_sums = jnp.sum(grad_inputs, axis=1)
    col_sums = jnp.sum(grad_inputs, axis=0)
    summand = jnp.zeros((tokens, 2 * channels), jnp.float32)
    summand = lax.dynamic_update_slice(summand, row_sums, (pair_index * row_count, 0))
    summand = lax.dynamic_update_slice(summand, col_sums, (atom_index * col_count, channels))
    totals = lax.psum(summand, ("pair", "atom"))
    left_total = totals[:, :channels]
    right_total = totals[:, channels:]
    single_grad = (
        jnp.dot(left_total, left_weight.astype(jnp.float32).T, precision=HIGHEST)
        + jnp.dot(right_total, right_weight.astype(jnp.float32).T, precision=HIGHEST)
    ).astype(jnp.bfloat16)
    picked = jnp.einsum("ta,tc->ac", member, single_grad, preferred_element_type=jnp.float32)
    atom_counts = jnp.einsum("ta,t->a", member, counts_all, preferred_element_type=jnp.float32)
    safe_counts = jnp.where(live_slot, atom_counts, jnp.float32(1.0))
    hidden_grad = picked / safe_counts[:, None]
    atom_sigmoid = jax.nn.sigmoid(atom_pre)
    pre_grad = (hidden_grad * atom_sigmoid * (1.0 + atom_pre * (1.0 - atom_sigmoid))).astype(
        jnp.bfloat16
    )
    atom_grad = jnp.einsum(
        "ac,fc->af", pre_grad, atom_weight, preferred_element_type=jnp.float32
    ).astype(jnp.bfloat16)
    return (pair_grad, atom_grad)


def solution(mesh):
    placed = (
        P("pair", "atom", None),
        P("pair", "atom", None),
        P(("pair", "atom"), None),
        P(("pair", "atom")),
        P(("pair", "atom")),
        P(),
        P(),
        P(),
        P(),
        P(),
    )
    return jax.shard_map(
        body,
        mesh=mesh,
        in_specs=placed,
        out_specs=(P("pair", "atom", None), P(("pair", "atom"), None)),
        check_vma=False,
    )
```

profile of v0, /device:TPU:1, one launch (start us, length us, event | category | flops | bytes accessed | tf_op | source)
XLA Modules:
  0.0 361.7 jit_solution(5642291847806016171)
XLA Ops:
  7.2 0.7 copy-done.19
  8.0 0.7 copy-done.18
  9.3 6.2 %collective-permute-start.1 = (f32[1]{0:T(128)}, f32[1]{0:T(128)}, u32[]{:S(2)}, u32[]{:S(2)}) collective-permute-start(f32[1]{0:T(128)} %bitcast.1), channel_id=1, source_target_pairs={{1,0},{2,1},{3,2},{4,3},{5,4},{6,5},{7,6},{8,7},{9,8},{10,9},{11,1... | collective-permute-start | bytes 20 | tf_op jit(solution)/shard_map/ppermute | solution.py:13
  15.5 1.8 multiply_convert_fusion.2
  17.3 2.6 collective-permute-start
  20.5 0.7 fusion.147
  22.4 60.1 %all-gather = bf16[128,4,256]{2,1,0:T(4,128)(2,1)S(1)} all-gather(bf16[1,4,256]{2,1,0:T(4,128)(2,1)S(1)} %maximum_bitcast_fusion.1), channel_id=1, replica_groups=mesh['pair'=32,'atom'=4] {'pair','atom'}, dimensions={0}, use_global_device_ids=true | all-gather | bytes 264192 | tf_op jit(solution)/shard_map/all_gather | solution.py:104
  84.0 0.7 convolution_bitcast_fusion.1
  84.7 0.7 fusion.8
  85.5 0.7 convolution_bitcast_fusion.2
  86.2 0.7 fusion.5
  87.5 1.1 maximum_bitcast_fusion
  88.6 2.7 copy.106
  91.3 25.4 %all_to_all.20 = bf16[2,128,1,16,128]{4,3,0,2,1:T(8,128)(2,1)S(1)} all-to-all(bf16[2,128,1,16,128]{4,3,0,2,1:T(8,128)(2,1)} %copy.106), channel_id=1, replica_groups=mesh['pair'=32,'atom'=4] {'pair','atom'}, dimensions={1} | all-to-all | bytes 2097152 | tf_op jit(solution)/shard_map/all_to_all | solution.py:36
  118.4 1.3 convolution_convert_fusion.2
  119.6 1.2 reshape_broadcast_in_dim.6
  120.8 0.9 copy.110
  121.7 3.8 %all-to-all-start.1 = ((bf16[1,128,1,16,128]{4,3,2,0,1:T(8,128)(2,1)}), bf16[1,128,1,16,128]{4,3,2,0,1:T(8,128)(2,1)S(1)}, u32[]{:S(2)}, u32[]{:S(2)}) async-start(bf16[1,128,1,16,128]{4,3,2,0,1:T(8,128)(2,1)} %bitcast.160), calls=%async_computation.1 | async-start | bytes 1048576 | tf_op jit(solution)/shard_map/all_to_all | solution.py:53
  125.5 2.5 fusion.10
  128.0 11.4 %all-to-all-done.1 = bf16[1,128,1,16,128]{4,3,2,0,1:T(8,128)(2,1)S(1)} async-done(((bf16[1,128,1,16,128]{4,3,2,0,1:T(8,128)(2,1)}), bf16[1,128,1,16,128]{4,3,2,0,1:T(8,128)(2,1)S(1)}, u32[]{:S(2)}, u32[]{:S(2)}) %all-to-all-start.1) | async-done | bytes 524320 | tf_op jit(solution)/shard_map/all_to_all | solution.py:53
  139.7 0.9 copy-done.5
  140.6 1.4 fusion.146
  142.8 17.5 %all_to_all.21 = bf16[1,128,1,16,128]{4,3,2,0,1:T(8,128)(2,1)S(1)} all-to-all(bf16[1,128,1,16,128]{4,3,2,0,1:T(8,128)(2,1)S(1)} %copy.114), channel_id=1, replica_groups=mesh['pair'=32,'atom'=4] {'pair','atom'}, dimensions={1} | all-to-all | bytes 1048576 | tf_op jit(solution)/shard_map/all_to_all | solution.py:36
  160.5 0.8 copy-done.13
  161.3 1.3 convolution_convert_fusion.1
  162.6 1.3 convolution_convert_fusion
  163.8 2.0 stack.21
  165.8 1.9 copy.116
  167.7 2.0 stack.22
  169.7 1.2 copy.117
  171.0 1.2 copy.118
  172.2 5.0 %all-to-all-start.3 = ((bf16[2,128,1,16,128]{4,3,2,0,1:T(8,128)(2,1)}), bf16[2,128,1,16,128]{4,3,2,0,1:T(8,128)(2,1)}, u32[]{:S(2)}, u32[]{:S(2)}) async-start(bf16[2,128,1,16,128]{4,3,2,0,1:T(8,128)(2,1)} %copy.118), calls=%async_computation.3 | async-start | bytes 2097152 | tf_op jit(solution)/shard_map/all_to_all | solution.py:53
  177.3 3.0 fusion.15
  180.3 16.2 %all-to-all-done.3 = bf16[2,128,1,16,128]{4,3,2,0,1:T(8,128)(2,1)} async-done(((bf16[2,128,1,16,128]{4,3,2,0,1:T(8,128)(2,1)}), bf16[2,128,1,16,128]{4,3,2,0,1:T(8,128)(2,1)}, u32[]{:S(2)}, u32[]{:S(2)}) %all-to-all-start.3) | async-done | bytes 1048608 | tf_op jit(solution)/shard_map/all_to_all | solution.py:53
  196.4 2.4 fusion.150
  198.8 1.5 copy.139
  200.2 1.6 convolution_add_fusion.3
  201.9 2.2 convolution_add_fusion.2
  204.1 1.5 copy.140
  205.7 1.2 convolution_add_fusion.1
  206.9 1.4 fusion.145
  208.4 0.7 fusion.137
  209.2 0.8 copy-done.7
  210.3 63.4 %all-reduce = bf16[512]{0:T(512)(128)(2,1)S(1)} all-reduce(bf16[512]{0:T(512)(128)(2,1)S(1)} %dynamic-update-slice), channel_id=1, replica_groups=mesh['pair'=32,'atom'=4] {'pair','atom'}, use_global_device_ids=true, to_apply=%add | all-reduce | flops 512 | bytes 2048
  273.9 1.0 copy.126
  274.9 76.4 %all-reduce.3.cloned.1.call-done = f32[512,256]{1,0:T(8,128)} async-done(((f32[512,256]{1,0:T(8,128)}), f32[512,256]{1,0:T(8,128)}) %all-reduce.3.cloned.1.call-update) | async-done | bytes 524304 | tf_op jit(solution)/shard_map/psum | solution.py:189
  351.3 1.5 fusion.83
  353.8 1.0 fusion.20
  (92 shorter events, 9.3 us)
Async XLA Ops:
  7.2 15.1 %copy-start = (bf16[384,128]{1,0:T(8,128)(2,1)S(1)}, bf16[384,128]{1,0:T(8,128)(2,1)}, u32[]{:S(2)}) copy-start(bf16[384,128]{1,0:T(8,128)(2,1)} %param.18) | copy-start | bytes 294916
  7.2 0.7 copy-start.19
  8.0 0.7 copy-start.18
  9.3 10.9 %copy-start.9 = (bf16[16,128,128]{2,1,0:T(8,128)(2,1)S(1)}, bf16[16,128,128]{2,1,0:T(8,128)(2,1)}, u32[]{:S(2)}) copy-start(bf16[16,128,128]{2,1,0:T(8,128)(2,1)} %param.10) | copy-start | bytes 1572868
  9.3 11.2 %collective-permute-start.1 = (f32[1]{0:T(128)}, f32[1]{0:T(128)}, u32[]{:S(2)}, u32[]{:S(2)}) collective-permute-start(f32[1]{0:T(128)} %bitcast.1), channel_id=1, source_target_pairs={{1,0},{2,1},{3,2},{4,3},{5,4},{6,5},{7,6},{8,7},{9,8},{10,9},{11,1... | collective-permute-start | bytes 20 | tf_op jit(solution)/shard_map/ppermute | solution.py:13
  17.3 4.3 %collective-permute-start = (f32[1,384]{1,0:T(1,128)S(1)}, f32[1,384]{1,0:T(1,128)S(1)}, u32[]{:S(2)}, u32[]{:S(2)}) collective-permute-start(f32[1,384]{1,0:T(1,128)S(1)} %fusion.124), channel_id=1, source_target_pairs={{1,0},{2,1},{3,2},{4,3},{5,4},{6,5},{7,6},{8,7},{9,8},{10,9},{11,1... | collective-permute-start | bytes 4616 | tf_op jit(solution)/shard_map/ppermute | solution.py:13
  21.2 0.9 copy-start.15
  83.1 0.9 copy-start.16
  84.7 2.2 copy-start.1
  86.2 1.0 copy-start.3
  117.3 0.8 copy-start.10
  117.5 0.8 copy-start.12
  121.7 17.7 %all-to-all-start.1 = ((bf16[1,128,1,16,128]{4,3,2,0,1:T(8,128)(2,1)}), bf16[1,128,1,16,128]{4,3,2,0,1:T(8,128)(2,1)S(1)}, u32[]{:S(2)}, u32[]{:S(2)}) async-start(bf16[1,128,1,16,128]{4,3,2,0,1:T(8,128)(2,1)} %bitcast.160), calls=%async_computation.1 | async-start | bytes 1048576 | tf_op jit(solution)/shard_map/all_to_all | solution.py:53
  139.4 1.2 copy-start.5
  139.5 1.1 copy-start.17
  160.3 1.0 copy-start.13
  161.3 1.3 copy-start.11
  169.7 1.2 copy-start.8
  172.2 24.2 %all-to-all-start.3 = ((bf16[2,128,1,16,128]{4,3,2,0,1:T(8,128)(2,1)}), bf16[2,128,1,16,128]{4,3,2,0,1:T(8,128)(2,1)}, u32[]{:S(2)}, u32[]{:S(2)}) async-start(bf16[2,128,1,16,128]{4,3,2,0,1:T(8,128)(2,1)} %copy.118), calls=%async_computation.3 | async-start | bytes 2097152 | tf_op jit(solution)/shard_map/all_to_all | solution.py:53
  177.2 174.1 %all-reduce.3.cloned.1.call-start = ((), (), s32[]{:S(2)}) async-start(), calls=%async_computation.4 | async-start | bytes 1048576 | tf_op jit(solution)/shard_map/psum | solution.py:189
  200.2 1.7 copy-start.4
  204.1 1.6 copy-start.6
  205.7 1.2 copy-start.2
  209.2 0.8 copy-start.7
  351.3 1.5 copy-start.14
  352.8 0.9 copy-start.20
  352.9 1.0 copy-start.21
Sparse Core Ops, SparseCore 0:
  210.2 141.0 all-reduce.2
where the time goes:
time: 363 us; the launch traced here: 362 us
  blocking collectives  166 us (46%)
  waiting for transfers between devices  104 us (29%)
  local copies, waits for them, and re-layouts  28.1 us (8%)
  matrix products  25.5 us (7%)
  starting transfers between devices  17.7 us (5%)
  between operations  14.6 us (4%)
  other arithmetic  5.05 us (1%)
    psum x1, waiting for transfers between devices, body(): totals = lax.psum(summand, ('pair', 'atom'))  76.4 us
    unnamed x1, blocking collectives  63.4 us
    all_gather x1, blocking collectives, body(): lax.all_gather(jnp.concatenate([left_own, right_own], axis=1), ('pair', '...  60.1 us
    all_to_all x2, blocking collectives, to_channels(): lax.all_to_all(shaped, ('pair', 'atom'), split_axis=1, concat_axis=1, til...  42.8 us
    all_to_all x2, waiting for transfers between devices, to_pairs(): lax.all_to_all(shaped, ('pair', 'atom'), split_axis=1, concat_axis=1, til...  27.6 us
    unnamed x53, local copies, waits for them, and re-layouts  11 us
    all_to_all x2, starting transfers between devices, to_pairs(): lax.all_to_all(shaped, ('pair', 'atom'), split_axis=1, concat_axis=1, til...  8.82 us
    ppermute x2, starting transfers between devices, shifted_2(): return lax.ppermute(x, axis, pairs)  8.8 us
  transfers between devices with their start and end apart: 5, of which 4 were waited for; matrix products, arithmetic and copies ran while one was open for 3% of the time, Pallas kernels for 0%

commit v1 on v0

v1 whole, which is shorter than its diff:
```python
import jax
import jax.numpy as jnp
from jax import lax
from jax.experimental import pallas as pl
from jax.experimental.pallas import tpu as pltpu
from jax.sharding import PartitionSpec as P

EPSILON = 1e-05
F32 = jnp.float32
BF16 = jnp.bfloat16
ROWS = 16
COLS = 128
CH = 128
DEV = 128
TOK = 512
WIN = 32
PAIR_DEV = 32
ATOM_DEV = 4
CHUNK = 32


def dot_nn(a, b):
    return lax.dot_general(a, b, (((1,), (0,)), ((), ())), preferred_element_type=F32)


def dot_nt(a, b):
    return lax.dot_general(a, b, (((1,), (1,)), ((), ())), preferred_element_type=F32)


def dot_tn(a, b):
    return lax.dot_general(a, b, (((0,), (0,)), ((), ())), preferred_element_type=F32)


def split(x):
    high = x.astype(BF16)
    return high, (x - high.astype(F32)).astype(BF16)


def sigmoid(x):
    return 0.5 * jnp.tanh(0.5 * x) + 0.5


def loop(start, stop, step):
    def run(i, carry):
        step(i)
        return carry

    lax.fori_loop(start, stop, run, 0)


def kernel(
    pair_ref,
    cot_ref,
    feat_ref,
    tok_ref,
    count_ref,
    iw_ref,
    ow_ref,
    aw_ref,
    lw_ref,
    rw_ref,
    pg_ref,
    ag_ref,
    member_ref,
    dsilu_ref,
    bias_msg,
    right_in,
    left_in,
    right_bias,
    right_inv,
    left_bias,
    left_inv,
    wt_ref,
    wt5_ref,
    mt_ref,
    normed_ref,
    inv_ref,
    hidden_ref,
    sig_left,
    sig_right,
    der_left,
    der_right,
    gate_ref,
    gn_ref,
    gg_ref,
    work_a,
    work_b,
    edge_out,
    edge_in,
    prod_out,
    prod_in,
    gp_out,
    gp_in,
    grad_out,
    grad_in,
    col_acc,
    row_ext,
    col_ext,
    row_msg,
    col_msg,
    row_in,
    col_in,
    send_sem,
    recv_sem,
):
    pos = lax.axis_index("pair")
    y = lax.axis_index("atom")
    me = pos * ATOM_DEV + y
    z = pos // 8
    x = (pos // 2) % 4
    c = pos % 2

    def remote(src, dst, sem, p, a):
        pltpu.make_async_remote_copy(
            src_ref=src,
            dst_ref=dst,
            send_sem=send_sem.at[sem],
            recv_sem=recv_sem.at[sem],
            device_id=(p, a),
            device_id_type=pl.DeviceIdType.MESH,
        ).start()

    def local(src, dst, sem):
        pltpu.make_async_copy(src, dst, recv_sem.at[sem]).start()

    def either(src, dst, sem, p, a, is_self):
        @pl.when(is_self)
        def _():
            local(src, dst, sem)

        @pl.when(jnp.logical_not(is_self))
        def _():
            remote(src, dst, sem, p, a)

    def wait_recv(ref, sem):
        pltpu.make_async_copy(ref, ref, recv_sem.at[sem]).wait()

    def wait_send(ref, sem):
        pltpu.make_async_copy(ref, ref, send_sem.at[sem]).wait()

    def plane(step):
        return (z + step) % 4

    def send_plane(step, zc, send_one, self_one):
        def one(q):
            p = zc * 8 + ((x + q // 8) % 4) * 2 + (c + q % 2) % 2
            a = (y + (q // 2) % 4) % 4
            send_one(p, a)

        if step == 0:
            self_one()
            loop(1, CHUNK, one)
        else:
            loop(0, CHUNK, one)

    atom_pre = dot_nn(feat_ref[...], aw_ref[...])
    atom_sig = sigmoid(atom_pre)
    atom_hidden = (atom_pre * atom_sig).astype(BF16)
    dsilu_ref[...] = atom_sig * (1.0 + atom_pre * (1.0 - atom_sig))
    slot = lax.broadcasted_iota(jnp.int32, (1, DEV), 1)
    live_count = jnp.full((1, DEV), 0, jnp.int32)
    for w in range(4):
        live_count = jnp.where(slot // WIN == w, count_ref[w], live_count)
    live = slot % WIN < live_count
    row8 = lax.broadcasted_iota(jnp.int32, (8, DEV), 0)
    lane8 = lax.broadcasted_iota(jnp.int32, (8, DEV), 1)
    member = jnp.where(
        (tok_ref[...] == me * 4 - 1 + row8) & (row8 < 5) & live, F32(1.0), F32(0.0)
    )
    member_ref[...] = member
    high, low = split(dot_nn(member.astype(BF16), atom_hidden))
    counts = jnp.sum(member, axis=1, keepdims=True)
    count_row = jnp.sum(jnp.where(lane8 == row8, counts, 0.0), axis=0, keepdims=True)
    for n, w_ref in enumerate((lw_ref, rw_ref)):
        weight = w_ref[...]
        sums = dot_nn(high, weight) + dot_nn(low, weight)
        bias_msg[n] = jnp.where(row8 == 5, count_row, sums)

    block = me // PAIR_DEV
    place = me % PAIR_DEV
    right_src = bias_msg.at[1]
    right_dst = right_in.at[pl.ds(pl.multiple_of(place * 8, 8), 8)]
    right_self = block == y
    either(right_src, right_dst, 0, pos, block, right_self)
    loop(1, PAIR_DEV, lambda q: remote(right_src, right_dst, 0, (pos + q) % PAIR_DEV, block))
    right_lead = (place == 0) & (me > 0)
    right_lead_self = right_lead & (block - 1 == y)

    @pl.when(right_lead)
    def _():
        lead_dst = right_in.at[pl.ds(PAIR_DEV * 8, 8)]
        either(right_src, lead_dst, 1, pos, block - 1, block - 1 == y)
        loop(
            1, PAIR_DEV, lambda q: remote(right_src, lead_dst, 1, (pos + q) % PAIR_DEV, block - 1)
        )

    left_src = bias_msg.at[0]
    left_dst = left_in.at[pl.ds(pl.multiple_of(y * 8, 8), 8)]
    local(left_src, left_dst, 2)
    loop(1, ATOM_DEV, lambda q: remote(left_src, left_dst, 2, pos, (y + q) % ATOM_DEV))
    left_lead = (y == 0) & (pos > 0)

    @pl.when(left_lead)
    def _():
        loop(
            0,
            ATOM_DEV,
            lambda q: remote(
                left_src, left_in.at[pl.ds(ATOM_DEV * 8, 8)], 3, pos - 1, (y + q) % ATOM_DEV
            ),
        )

    for q in range(4):
        turned = iw_ref[:, q * CH : (q + 1) * CH].astype(F32).T.astype(BF16)
        for zc in range(4):
            wt_ref[zc, q * CHUNK : (q + 1) * CHUNK, :] = turned[zc * CHUNK : (zc + 1) * CHUNK, :]
    wt5_ref[...] = iw_ref[:, 4 * CH :].astype(F32).T.astype(BF16)
    mt_ref[...] = ow_ref[...].astype(F32).T.astype(BF16)

    @pl.when(y == ATOM_DEV - 1)
    def _():
        right_in[pl.ds(PAIR_DEV * 8, 8), :] = jnp.zeros((8, CH), F32)

    @pl.when(pos == PAIR_DEV - 1)
    def _():
        left_in[pl.ds(ATOM_DEV * 8, 8), :] = jnp.zeros((8, CH), F32)

    wait_recv(right_in.at[pl.ds(0, PAIR_DEV * 8)], 0)

    @pl.when(y < ATOM_DEV - 1)
    def _():
        wait_recv(right_in.at[pl.ds(PAIR_DEV * 8, 8)], 1)

    wait_recv(left_in.at[pl.ds(0, ATOM_DEV * 8)], 2)

    @pl.when(pos < PAIR_DEV - 1)
    def _():
        wait_recv(left_in.at[pl.ds(ATOM_DEV * 8, 8)], 3)

    def finish_bias(src, bias_ref, inverse_ref, n):
        lane = lax.broadcasted_iota(jnp.int32, (n, CH), 1)
        count_own = src[pl.ds(5, n, stride=8), :]
        count_next = src[pl.ds(13, n, stride=8), :]
        for q in range(4):
            total = src[pl.ds(1 + q, n, stride=8), :]
            number = jnp.where(lane == 1 + q, count_own, 0.0)
            if q == 3:
                total = total + src[pl.ds(8, n, stride=8), :]
                number = number + jnp.where(lane == 0, count_next, 0.0)
            inverse = 1.0 / jnp.sum(number, axis=1, keepdims=True)
            bias_ref[pl.ds(q, n, stride=4), :] = (total * inverse).astype(BF16).astype(F32)
            inverse_ref[pl.ds(q, n, stride=4), :] = jnp.broadcast_to(inverse, (n, CH))

    finish_bias(right_in, right_bias, right_inv, PAIR_DEV)
    finish_bias(left_in, left_bias, left_inv, ATOM_DEV)

    def front(r):
        values = pair_ref[r].astype(F32) + left_bias[pl.ds(r, 1), :] + right_bias[...]
        values = values.T
        centre = jnp.mean(values, axis=0, keepdims=True)
        shifted = values - centre
        inverse = lax.rsqrt(jnp.mean(shifted * shifted, axis=0, keepdims=True) + EPSILON)
        normed = shifted * inverse
        normed_ref[r] = normed
        inv_ref[pl.ds(r, 1), :] = inverse
        hidden_ref[r] = normed.astype(BF16)

    loop(0, ROWS, front)

    edge_dst = edge_in.at[:, y, pl.ds(pl.multiple_of(pos * ROWS, ROWS), ROWS)]
    for step in range(4):
        zc = plane(step)
        first = pl.multiple_of(zc * CHUNK, CHUNK)

        def edges(r):
            pre = dot_nn(wt_ref[zc], hidden_ref[r])
            left_sig = sigmoid(pre[CHUNK : 2 * CHUNK])
            right_sig = sigmoid(pre[3 * CHUNK :])
            left = left_sig * pre[:CHUNK]
            right = right_sig * pre[2 * CHUNK : 3 * CHUNK]
            work_a[pl.ds(r, CHUNK, stride=ROWS), :] = left
            work_b[pl.ds(r, CHUNK, stride=ROWS), :] = right
            sig_left[r, pl.ds(first, CHUNK), :] = left_sig
            sig_right[r, pl.ds(first, CHUNK), :] = right_sig
            der_left[r, pl.ds(first, CHUNK), :] = left * (1.0 - left_sig)
            der_right[r, pl.ds(first, CHUNK), :] = right * (1.0 - right_sig)

        loop(0, ROWS, edges)
        span = CHUNK * ROWS
        edge_out[0, pl.ds(first, CHUNK)] = (
            work_a[:span, :].reshape(CHUNK, ROWS, COLS).astype(BF16)
        )
        edge_out[1, pl.ds(first, CHUNK)] = (
            work_b[:span, :].reshape(CHUNK, ROWS, COLS).astype(BF16)
        )
        send_plane(
            step,
            zc,
            lambda p, a: remote(edge_out.at[:, p * 4 + a], edge_dst, 4, p, a),
            lambda: local(edge_out.at[:, me], edge_dst, 4),
        )

    def gate(r):
        opened = sigmoid(dot_nn(wt5_ref[...], hidden_ref[r]))
        gated = cot_ref[r].astype(F32).T * opened
        gate_ref[r] = gated * (1.0 - opened)
        gn_ref[pl.ds(r, CH, stride=ROWS), :] = dot_nn(ow_ref[...], gated.astype(BF16))

    loop(0, ROWS, gate)

    def total(i, acc):
        chunk = gn_ref[pl.ds(pl.multiple_of(i * 128, 128), 128), :].reshape(8, ROWS, COLS)
        return acc + jnp.sum(chunk, axis=0)

    zero = jnp.zeros((ROWS, COLS), F32)
    gn_mean = lax.fori_loop(0, 16, total, zero) * (1.0 / CH)

    wait_recv(edge_in, 4)

    prod_dst = prod_in.at[me]
    for step in range(4):
        zc = plane(step)
        first = pl.multiple_of(zc * 128, 128)
        product = dot_nt(edge_in[0, 0, pl.ds(first, 128), :], edge_in[1, 0])
        for a in range(1, 4):
            product = product + dot_nt(edge_in[0, a, pl.ds(first, 128), :], edge_in[1, a])
        for a in range(4):
            prod_out[a, pl.ds(first, 128), :] = product[:, a * 128 : (a + 1) * 128].astype(BF16)

        def block_of(ref, p, a):
            return ref.at[a, pl.ds(pl.multiple_of(p * ROWS, ROWS), ROWS)]

        send_plane(
            step,
            zc,
            lambda p, a: remote(block_of(prod_out, p, a), prod_dst, 5, p, a),
            lambda: local(block_of(prod_out, pos, y), prod_dst, 5),
        )
    wait_recv(prod_in, 5)

    def sum_prod(i, acc):
        return acc + jnp.sum(prod_in[pl.ds(i * 8, 8)].astype(F32), axis=0)

    prod_mean = lax.fori_loop(0, 16, sum_prod, zero) * (1.0 / CH)

    def sum_squares(i, carry):
        squares, cross = carry
        shifted = prod_in[pl.ds(i * 8, 8)].astype(F32) - prod_mean[None]
        upstream = gn_ref[pl.ds(pl.multiple_of(i * 128, 128), 128), :].reshape(8, ROWS, COLS)
        return (
            squares + jnp.sum(shifted * shifted, axis=0),
            cross + jnp.sum(upstream * shifted, axis=0),
        )

    squares, cross = lax.fori_loop(0, 16, sum_squares, (zero, zero))
    prod_inv = lax.rsqrt(squares * (1.0 / CH) + EPSILON)
    cross = cross * prod_inv * prod_inv * (1.0 / CH)

    gp_dst = gp_in.at[y, pl.ds(pl.multiple_of(pos * ROWS, ROWS), ROWS)]
    for step in range(4):
        zc = plane(step)

        def grads(i):
            at = zc * CHUNK + i * 8
            shifted = prod_in[pl.ds(at, 8)].astype(F32) - prod_mean[None]
            upstream = gn_ref[pl.ds(pl.multiple_of(at * ROWS, 128), 128), :]
            upstream = upstream.reshape(8, ROWS, COLS)
            grad = prod_inv[None] * (upstream - gn_mean[None] - shifted * cross[None])
            gp_out[pl.ds(at, 8)] = grad.astype(BF16)

        loop(0, 4, grads)
        send_plane(
            step,
            zc,
            lambda p, a: remote(gp_out.at[p * 4 + a], gp_dst, 6, p, a),
            lambda: local(gp_out.at[me], gp_dst, 6),
        )

    def lay_normed(i):
        shifted = (prod_in[pl.ds(i * 8, 8)].astype(F32) - prod_mean[None]) * prod_inv[None]
        work_a[pl.ds(pl.multiple_of(i * 128, 128), 128), :] = shifted.reshape(128, COLS)

    loop(0, 16, lay_normed)

    def gate_grad(r):
        normed = work_a[pl.ds(r, CH, stride=ROWS), :].astype(BF16)
        gg_ref[r] = (dot_nn(mt_ref[...], normed) * gate_ref[r]).astype(BF16)

    loop(0, ROWS, gate_grad)

    wait_recv(gp_in, 6)

    for side in range(2):
        grad_dst = grad_in.at[side, me]
        for step in range(4):
            zc = plane(step)
            first = pl.multiple_of(zc * 128, 128)
            if side == 0:
                lhs = jnp.concatenate([gp_in[a, pl.ds(first, 128), :] for a in range(4)], axis=1)
            else:
                lhs = gp_in[zc].T
            for a in range(4):
                grad_out[side, a, pl.ds(first, 128), :] = dot_nn(
                    lhs, edge_in[1 - side, a]
                ).astype(BF16)

            def grad_block(p, a):
                return grad_out.at[side, a, pl.ds(pl.multiple_of(p * ROWS, ROWS), ROWS)]

            send_plane(
                step,
                zc,
                lambda p, a: remote(grad_block(p, a), grad_dst, 7 + side, p, a),
                lambda: local(grad_block(pos, y), grad_dst, 7 + side),
            )

    row_ext[...] = jnp.zeros_like(row_ext)
    col_ext[...] = jnp.zeros_like(col_ext)
    col_acc[...] = jnp.zeros_like(col_acc)

    for side, work in ((0, work_a), (1, work_b)):
        wait_recv(grad_in.at[side], 7 + side)

        def lay_grads(i):
            work[pl.ds(pl.multiple_of(i * 128, 128), 128), :] = (
                grad_in[side, pl.ds(i * 8, 8)].astype(F32).reshape(128, COLS)
            )

        loop(0, 16, lay_grads)

    def last(r):
        left = work_a[pl.ds(r, CH, stride=ROWS), :]
        right = work_b[pl.ds(r, CH, stride=ROWS), :]
        branches = jnp.concatenate(
            [
                (left * sig_left[r]).astype(BF16),
                (left * der_left[r]).astype(BF16),
                (right * sig_right[r]).astype(BF16),
                (right * der_right[r]).astype(BF16),
                gg_ref[r],
            ],
            axis=0,
        )
        grad = dot_nn(iw_ref[...], branches)
        normed = normed_ref[r]
        first_mean = jnp.mean(grad, axis=0, keepdims=True)
        cross_mean = jnp.mean(grad * normed, axis=0, keepdims=True)
        grad = inv_ref[pl.ds(r, 1), :] * (grad - first_mean - normed * cross_mean)
        grad = grad.T
        pg_ref[r] = grad.astype(BF16)
        col_acc[...] += grad
        row_ext[pl.ds(8 + r, 1), :] = jnp.sum(grad, axis=0, keepdims=True)

    loop(0, ROWS, last)

    row_ext[8:24, :] = row_ext[8:24, :] * left_inv[...]
    col_ext[8:136, :] = col_acc[...] * right_inv[...]
    for m in range(ATOM_DEV + 1):
        row_msg[m] = row_ext[7 + 4 * m : 15 + 4 * m, :]
    for m in range(PAIR_DEV + 1):
        col_msg[m] = col_ext[7 + 4 * m : 15 + 4 * m, :]

    local(row_msg.at[y], row_in.at[y], 9)

    def send_row(q):
        a = (y + q) % ATOM_DEV
        remote(row_msg.at[a], row_in.at[y], 9, pos, a)

    loop(1, ATOM_DEV, send_row)
    row_lead = pos < PAIR_DEV - 1

    @pl.when(row_lead)
    def _():
        remote(row_msg.at[ATOM_DEV], row_in.at[ATOM_DEV + y], 10, pos + 1, 0)

    def send_col(q):
        m = (place + q) % PAIR_DEV
        p = y * 8 + m // 4
        a = m % 4
        either(col_msg.at[m], col_in.at[pos], 11, p, a, (p == pos) & (a == y))

    loop(0, PAIR_DEV, send_col)
    col_lead = y < ATOM_DEV - 1
    col_lead_self = col_lead & (pos == (y + 1) * 8) & (y == 0)

    @pl.when(col_lead)
    def _():
        either(
            col_msg.at[PAIR_DEV],
            col_in.at[PAIR_DEV + pos],
            12,
            (y + 1) * 8,
            0,
            col_lead_self,
        )

    row_more = (y == 0) & (pos > 0)
    col_more = (place == 0) & (me > 0)

    @pl.when(jnp.logical_not(row_more))
    def _():
        row_in[ATOM_DEV:] = jnp.zeros((ATOM_DEV, 8, CH), F32)

    @pl.when(jnp.logical_not(col_more))
    def _():
        col_in[PAIR_DEV:] = jnp.zeros((PAIR_DEV, 8, CH), F32)

    wait_recv(row_in.at[pl.ds(0, ATOM_DEV)], 9)

    @pl.when(row_more)
    def _():
        wait_recv(row_in.at[pl.ds(ATOM_DEV, ATOM_DEV)], 10)

    wait_recv(col_in.at[pl.ds(0, PAIR_DEV)], 11)

    @pl.when(col_more)
    def _():
        wait_recv(col_in.at[pl.ds(PAIR_DEV, PAIR_DEV)], 12)

    single = jnp.zeros((8, 3 * CH), F32)
    for ref, w_ref in ((row_in, lw_ref), (col_in, rw_ref)):
        weight = w_ref[...]
        for part in split(jnp.sum(ref[...], axis=0)):
            single = single + dot_nt(part, weight)
    picked = dot_tn(member_ref[...].astype(BF16), single.astype(BF16))
    atom_grad = (picked * dsilu_ref[...]).astype(BF16)
    ag_ref[...] = dot_nt(atom_grad, aw_ref[...]).astype(BF16)

    wait_send(right_in.at[pl.ds(0, (PAIR_DEV - 1) * 8)], 0)

    @pl.when(jnp.logical_not(right_self))
    def _():
        wait_send(right_in.at[pl.ds(0, 8)], 0)

    @pl.when(right_lead)
    def _():
        wait_send(right_in.at[pl.ds(0, (PAIR_DEV - 1) * 8)], 1)

        @pl.when(jnp.logical_not(right_lead_self))
        def _():
            wait_send(right_in.at[pl.ds(0, 8)], 1)

    wait_send(left_in.at[pl.ds(0, (ATOM_DEV - 1) * 8)], 2)

    @pl.when(left_lead)
    def _():
        wait_send(left_in.at[pl.ds(0, ATOM_DEV * 8)], 3)

    wait_send(edge_out.at[:, pl.ds(0, DEV - 1)], 4)
    wait_send(prod_in.at[pl.ds(0, DEV - 1)], 5)
    wait_send(gp_out.at[pl.ds(0, DEV - 1)], 6)
    for side in range(2):
        wait_send(grad_in.at[side, pl.ds(0, DEV - 1)], 7 + side)
    wait_send(row_msg.at[pl.ds(0, ATOM_DEV - 1)], 9)

    @pl.when(row_lead)
    def _():
        wait_send(row_msg.at[pl.ds(0, 1)], 10)

    wait_send(col_msg.at[pl.ds(0, PAIR_DEV - 1)], 11)

    @pl.when(block != y)
    def _():
        wait_send(col_msg.at[pl.ds(0, 1)], 11)

    @pl.when(col_lead & jnp.logical_not(col_lead_self))
    def _():
        wait_send(col_msg.at[pl.ds(0, 1)], 12)


def body(
    pair_state,
    cotangent,
    atom_feats,
    atom_token,
    window_count,
    input_weight,
    output_weight,
    atom_weight,
    left_weight,
    right_weight,
):
    vmem = pl.BlockSpec(memory_space=pltpu.VMEM)
    rows = (ROWS, CH, COLS)
    scratch = [
        ((8, DEV), F32),
        ((DEV, 3 * CH), F32),
        ((2, 8, CH), F32),
        (((PAIR_DEV + 1) * 8 + 8, CH), F32),
        (((ATOM_DEV + 1) * 8 + 8, CH), F32),
        ((COLS, CH), F32),
        ((COLS, CH), F32),
        ((ROWS, CH), F32),
        ((ROWS, CH), F32),
        ((4, 4 * CHUNK, CH), BF16),
        ((CH, CH), BF16),
        ((CH, CH), BF16),
        (rows, F32),
        ((ROWS, COLS), F32),
        (rows, BF16),
        (rows, F32),
        (rows, F32),
        (rows, F32),
        (rows, F32),
        (rows, F32),
        ((CH * ROWS, COLS), F32),
        (rows, BF16),
        ((CH * ROWS, COLS), F32),
        ((CH * ROWS, COLS), F32),
        ((2, DEV, ROWS, COLS), BF16),
        ((2, 4, TOK, COLS), BF16),
        ((4, TOK, COLS), BF16),
        ((DEV, ROWS, COLS), BF16),
        ((DEV, ROWS, COLS), BF16),
        ((4, TOK, COLS), BF16),
        ((2, 4, TOK, COLS), BF16),
        ((2, DEV, ROWS, COLS), BF16),
        ((COLS, CH), F32),
        ((40, CH), F32),
        ((152, CH), F32),
        ((ATOM_DEV + 1, 8, CH), F32),
        ((PAIR_DEV + 1, 8, CH), F32),
        ((2 * ATOM_DEV, 8, CH), F32),
        ((2 * PAIR_DEV, 8, CH), F32),
    ]
    return pl.pallas_call(
        kernel,
        out_shape=(
            jax.ShapeDtypeStruct(pair_state.shape, BF16),
            jax.ShapeDtypeStruct(atom_feats.shape, BF16),
        ),
        in_specs=[
            vmem,
            vmem,
            vmem,
            vmem,
            pl.BlockSpec(memory_space=pltpu.SMEM),
            vmem,
            vmem,
            vmem,
            vmem,
            vmem,
        ],
        out_specs=(vmem, vmem),
        scratch_shapes=[pltpu.VMEM(shape, dtype) for shape, dtype in scratch]
        + [pltpu.SemaphoreType.DMA((13,)), pltpu.SemaphoreType.DMA((13,))],
        compiler_params=pltpu.CompilerParams(
            has_side_effects=True, vmem_limit_bytes=48 * 2**20
        ),
        cost_estimate=pl.CostEstimate(
            flops=1_700_000_000, bytes_accessed=2**21, transcendentals=2**20
        ),
    )(
        pair_state,
        cotangent,
        atom_feats,
        atom_token.reshape(1, -1),
        window_count,
        input_weight,
        output_weight,
        atom_weight,
        left_weight,
        right_weight,
    )


def solution(mesh):
    placed = (
        P("pair", "atom", None),
        P("pair", "atom", None),
        P(("pair", "atom"), None),
        P(("pair", "atom")),
        P(("pair", "atom")),
        P(),
        P(),
        P(),
        P(),
        P(),
    )
    return jax.shard_map(
        body,
        mesh=mesh,
        in_specs=placed,
        out_specs=(P("pair", "atom", None), P(("pair", "atom"), None)),
        check_vma=False,
    )
```

time: 363 us -> 114 us (0.31)
  blocking collectives: 166 us -> 0 us
  waiting for transfers between devices: 104 us -> 0 us
  Pallas kernels: 0 us -> 103 us
  matrix products: 25.5 us -> 0 us
  local copies, waits for them, and re-layouts: 28.1 us -> 9.25 us
  starting transfers between devices: 17.7 us -> 0 us
  between operations: 14.6 us -> 0.67 us
  other arithmetic: 5.05 us -> 0 us
    pallas_call x0 -> x1, Pallas kernels: none -> 103 us  [body(): pl.pallas_call(kernel, out_shape=(jax.ShapeDtypeStruct(pair_state.shape,...]
    psum x1 -> x0, waiting for transfers between devices: 76.4 us -> none  [body(): totals = lax.psum(summand, ('pair', 'atom'))]
    unnamed x1 -> x0, blocking collectives: 63.4 us -> none
    all_gather x1 -> x0, blocking collectives: 60.1 us -> none  [body(): lax.all_gather(jnp.concatenate([left_own, right_own], axis=1), ('pair', '...]
    all_to_all x2 -> x0, blocking collectives: 42.8 us -> none  [to_channels(): lax.all_to_all(shaped, ('pair', 'atom'), split_axis=1, concat_axis=1, til...]
    all_to_all x2 -> x0, waiting for transfers between devices: 27.6 us -> none  [to_pairs(): lax.all_to_all(shaped, ('pair', 'atom'), split_axis=1, concat_axis=1, til...]
    dot_general x23 -> x0, matrix products: 25.5 us -> none  [the longest x4 6.42 us: body(): jnp.einsum('hrk,ch->rkc', branch_grads[quarter], input_weight[:, quarter...]
    all_to_all x2 -> x0, starting transfers between devices: 8.82 us -> none  [to_pairs(): lax.all_to_all(shaped, ('pair', 'atom'), split_axis=1, concat_axis=1, til...]
  transfers between devices with their start and end apart: 5 -> 0, of which waited for: 4 -> 0; matrix products, arithmetic and copies ran while one was open for 3% -> 0% of each run, Pallas kernels for 0% -> 0%
where the time goes in v1:
time: 114 us; the launch traced here: 113 us
  Pallas kernels  103 us (90%)
  local copies, waits for them, and re-layouts  9.25 us (8%)
    pallas_call x1, Pallas kernels, body(): pl.pallas_call(kernel, out_shape=(jax.ShapeDtypeStruct(pair_state.shape,...  103 us
    unnamed x22, local copies, waits for them, and re-layouts  9.25 us

profile of v1, /device:TPU:1, one launch (start us, length us, event | category | flops | bytes accessed | tf_op | source)
XLA Modules:
  0.0 113.3 jit_solution(8392748473586780120)
XLA Ops:
  0.6 0.0 copy-start.9
  0.6 0.0 copy-start.8
  0.7 0.6 copy-done.9
  1.3 0.0 copy-done.8
  1.3 0.0 copy-start
  1.3 1.0 copy-done
  2.3 0.0 copy-start.1
  2.4 1.0 copy-done.1
  3.4 0.0 copy-start.2
  3.4 0.9 copy-done.2
  4.3 0.0 copy-start.3
  4.3 0.9 copy-done.3
  5.2 0.0 copy-start.4
  5.2 0.9 copy-done.4
  6.1 0.0 copy-start.5
  6.1 0.9 copy-done.5
  7.0 0.0 copy-start.6
  7.0 0.8 copy-done.6
  7.7 0.0 copy-start.7
  7.7 0.8 copy-done.7
  8.5 103.3 %shard_map.113 = (bf16[16,128,128]{2,1,0:T(8,128)(2,1)S(1)}, bf16[128,128]{1,0:T(8,128)(2,1)S(1)}) custom-call(bf16[16,128,128]{2,1,0:T(8,128)(2,1)S(1)} %copy-done, bf16[16,128,128]{2,1,0:T(8,128)(2,1)S(1)} %copy-done.1, bf16[128,128]{1,0:T(8,128)(2,1)S(1)} %copy-done.6, s32[1,128]{1,0:T(1,128)S(1)} %bitcast.1, s32[4]{0:T(128)S(1)} %copy-done.9, ...), custom_call_target="tpu_custom_call" | custom-call | flops 1700000000 | bytes 2097152 | tf_op jit(solution)/shard_map/pallas_call | solution.py:626
  111.9 0.8 copy.14
  112.6 0.6 copy.15
Async XLA Ops:
  0.6 0.7 copy-start.9
  0.6 0.7 copy-start.8
  1.3 1.0 copy-start
  2.3 1.0 copy-start.1
  3.4 0.9 copy-start.2
  4.3 0.9 copy-start.3
  5.2 0.9 copy-start.4
  6.1 0.9 copy-start.5
  7.0 0.8 copy-start.6
  7.7 0.8 copy-start.7

commit v2 on v1

--- a/solution.py
+++ b/solution.py
@@ -17,50 +17,53 @@
 PAIR_DEV = 32
 ATOM_DEV = 4
 CHUNK = 32
-
+UNROLL = 4
 
 def dot_nn(a, b):
     return lax.dot_general(a, b, (((1,), (0,)), ((), ())), preferred_element_type=F32)
 
-
 def dot_nt(a, b):
     return lax.dot_general(a, b, (((1,), (1,)), ((), ())), preferred_element_type=F32)
 
-
 def dot_tn(a, b):
     return lax.dot_general(a, b, (((0,), (0,)), ((), ())), preferred_element_type=F32)
-
 
 def split(x):
     high = x.astype(BF16)
     return high, (x - high.astype(F32)).astype(BF16)
 
-
 def sigmoid(x):
     return 0.5 * jnp.tanh(0.5 * x) + 0.5
 
-
-def loop(start, stop, step):
+def loop(start, stop, step, unroll=1):
     def run(i, carry):
         step(i)
         return carry
 
-    lax.fori_loop(start, stop, run, 0)
-
+    lax.fori_loop(start, stop, run, 0, unroll=unroll)
 
 def kernel(
+    pair_hbm,
+    cot_hbm,
+    feat_hbm,
+    tok_hbm,
+    count_ref,
+    iw_hbm,
+    ow_hbm,
+    aw_hbm,
+    lw_hbm,
+    rw_hbm,
+    pg_ref,
+    ag_ref,
     pair_ref,
     cot_ref,
     feat_ref,
     tok_ref,
-    count_ref,
     iw_ref,
     ow_ref,
     aw_ref,
     lw_ref,
     rw_ref,
-    pg_ref,
-    ag_ref,
     member_ref,
     dsilu_ref,
     bias_msg,
@@ -102,6 +105,7 @@
     col_in,
     send_sem,
     recv_sem,
+    load_sem,
 ):
     pos = lax.axis_index("pair")
     y = lax.axis_index("atom")
@@ -138,6 +142,25 @@
     def wait_send(ref, sem):
         pltpu.make_async_copy(ref, ref, send_sem.at[sem]).wait()
 
+    def channel(p, a):
+        return ((p // 8 + (p // 2) % 4 + a) % 4) * CHUNK + ((p // 2) % 4) * 8 + a * 2 + p % 2
+
+    mine = channel(pos, y)
+    group = (z + x + y) % 4
+
+    def send_group(step, send_one, self_one):
+        def one(q):
+            xs = (x + q // 8) % 4
+            a = (y + (q // 2) % 4) % 4
+            p = ((group + step - xs - a + 8) % 4) * 8 + xs * 2 + (c + q % 2) % 2
+            send_one(p, a)
+
+        if step == 0:
+            self_one()
+            loop(1, CHUNK, one)
+        else:
+            loop(0, CHUNK, one)
+
     def plane(step):
         return (z + step) % 4
 
@@ -152,6 +175,40 @@
             loop(1, CHUNK, one)
         else:
             loop(0, CHUNK, one)
+
+    barrier = pltpu.get_barrier_semaphore()
+
+    def greet(q):
+        to = (me + q) % DEV
+        pl.semaphore_signal(
+            barrier,
+            inc=1,
+            device_id=(to // ATOM_DEV, to % ATOM_DEV),
+            device_id_type=pl.DeviceIdType.MESH,
+        )
+
+    loop(1, DEV, greet)
+
+    loads = [
+        pltpu.make_async_copy(src, dst, load_sem.at[n])
+        for n, (src, dst) in enumerate(
+            (
+                (feat_hbm, feat_ref),
+                (aw_hbm, aw_ref),
+                (tok_hbm, tok_ref),
+                (lw_hbm, lw_ref),
+                (rw_hbm, rw_ref),
+                (iw_hbm, iw_ref),
+                (ow_hbm, ow_ref),
+                (pair_hbm, pair_ref),
+                (cot_hbm, cot_ref),
+            )
+        )
+    ]
+    for load in loads:
+        load.start()
+    for load in loads[:5]:
+        load.wait()
 
     atom_pre = dot_nn(feat_ref[...], aw_ref[...])
     atom_sig = sigmoid(atom_pre)
@@ -176,6 +233,17 @@
         sums = dot_nn(high, weight) + dot_nn(low, weight)
         bias_msg[n] = jnp.where(row8 == 5, count_row, sums)
 
+    for load in loads[5:]:
+        load.wait()
+    for q in range(4):
+        turned = iw_ref[:, q * CH : (q + 1) * CH].astype(F32).T.astype(BF16)
+        for zc in range(4):
+            wt_ref[zc, q * CHUNK : (q + 1) * CHUNK, :] = turned[zc * CHUNK : (zc + 1) * CHUNK, :]
+    wt5_ref[...] = iw_ref[:, 4 * CH :].astype(F32).T.astype(BF16)
+    mt_ref[...] = ow_ref[...].astype(F32).T.astype(BF16)
+
+    pl.semaphore_wait(barrier, DEV - 1)
+
     block = me // PAIR_DEV
     place = me % PAIR_DEV
     right_src = bias_msg.at[1]
@@ -209,13 +277,6 @@
                 left_src, left_in.at[pl.ds(ATOM_DEV * 8, 8)], 3, pos - 1, (y + q) % ATOM_DEV
             ),
         )
-
-    for q in range(4):
-        turned = iw_ref[:, q * CH : (q + 1) * CH].astype(F32).T.astype(BF16)
-        for zc in range(4):
-            wt_ref[zc, q * CHUNK : (q + 1) * CHUNK, :] = turned[zc * CHUNK : (zc + 1) * CHUNK, :]
-    wt5_ref[...] = iw_ref[:, 4 * CH :].astype(F32).T.astype(BF16)
-    mt_ref[...] = ow_ref[...].astype(F32).T.astype(BF16)
 
     @pl.when(y == ATOM_DEV - 1)
     def _():
@@ -265,11 +326,11 @@
         inv_ref[pl.ds(r, 1), :] = inverse
         hidden_ref[r] = normed.astype(BF16)
 
-    loop(0, ROWS, front)
+    loop(0, ROWS, front, UNROLL)
 
     edge_dst = edge_in.at[:, y, pl.ds(pl.multiple_of(pos * ROWS, ROWS), ROWS)]
     for step in range(4):
-        zc = plane(step)
+        zc = (group + step) % 4
         first = pl.multiple_of(zc * CHUNK, CHUNK)
 
         def edges(r):
@@ -285,7 +346,7 @@
             der_left[r, pl.ds(first, CHUNK), :] = left * (1.0 - left_sig)
             der_right[r, pl.ds(first, CHUNK), :] = right * (1.0 - right_sig)
 
-        loop(0, ROWS, edges)
+        loop(0, ROWS, edges, UNROLL)
         span = CHUNK * ROWS
         edge_out[0, pl.ds(first, CHUNK)] = (
             work_a[:span, :].reshape(CHUNK, ROWS, COLS).astype(BF16)
@@ -293,11 +354,10 @@
         edge_out[1, pl.ds(first, CHUNK)] = (
             work_b[:span, :].reshape(CHUNK, ROWS, COLS).astype(BF16)
         )
-        send_plane(
+        send_group(
             step,
-            zc,
-            lambda p, a: remote(edge_out.at[:, p * 4 + a], edge_dst, 4, p, a),
-            lambda: local(edge_out.at[:, me], edge_dst, 4),
+            lambda p, a: remote(edge_out.at[:, channel(p, a)], edge_dst, 4, p, a),
+            lambda: local(edge_out.at[:, mine], edge_dst, 4),
         )
 
     def gate(r):
@@ -306,7 +366,7 @@
         gate_ref[r] = gated * (1.0 - opened)
         gn_ref[pl.ds(r, CH, stride=ROWS), :] = dot_nn(ow_ref[...], gated.astype(BF16))
 
-    loop(0, ROWS, gate)
+    loop(0, ROWS, gate, UNROLL)
 
     def total(i, acc):
         chunk = gn_ref[pl.ds(pl.multiple_of(i * 128, 128), 128), :].reshape(8, ROWS, COLS)
@@ -317,7 +377,7 @@
 
     wait_recv(edge_in, 4)
 
-    prod_dst = prod_in.at[me]
+    prod_dst = prod_in.at[mine]
     for step in range(4):
         zc = plane(step)
         first = pl.multiple_of(zc * 128, 128)
@@ -336,6 +396,7 @@
             lambda p, a: remote(block_of(prod_out, p, a), prod_dst, 5, p, a),
             lambda: local(block_of(prod_out, pos, y), prod_dst, 5),
         )
+
     wait_recv(prod_in, 5)
 
     def sum_prod(i, acc):
@@ -358,7 +419,7 @@
 
     gp_dst = gp_in.at[y, pl.ds(pl.multiple_of(pos * ROWS, ROWS), ROWS)]
     for step in range(4):
-        zc = plane(step)
+        zc = (group + step) % 4
 
         def grads(i):
             at = zc * CHUNK + i * 8
@@ -369,11 +430,10 @@
             gp_out[pl.ds(at, 8)] = grad.astype(BF16)
 
         loop(0, 4, grads)
-        send_plane(
+        send_group(
             step,
-            zc,
-            lambda p, a: remote(gp_out.at[p * 4 + a], gp_dst, 6, p, a),
-            lambda: local(gp_out.at[me], gp_dst, 6),
+            lambda p, a: remote(gp_out.at[channel(p, a)], gp_dst, 6, p, a),
+            lambda: local(gp_out.at[mine], gp_dst, 6),
         )
 
     def lay_normed(i):
@@ -386,12 +446,12 @@
         normed = work_a[pl.ds(r, CH, stride=ROWS), :].astype(BF16)
         gg_ref[r] = (dot_nn(mt_ref[...], normed) * gate_ref[r]).astype(BF16)
 
-    loop(0, ROWS, gate_grad)
+    loop(0, ROWS, gate_grad, UNROLL)
 
     wait_recv(gp_in, 6)
 
     for side in range(2):
-        grad_dst = grad_in.at[side, me]
+        grad_dst = grad_in.at[side, mine]
         for step in range(4):
             zc = plane(step)
             first = pl.multiple_of(zc * 128, 128)
@@ -451,7 +511,7 @@
         col_acc[...] += grad
         row_ext[pl.ds(8 + r, 1), :] = jnp.sum(grad, axis=0, keepdims=True)
 
-    loop(0, ROWS, last)
+    loop(0, ROWS, last, UNROLL)
 
     row_ext[8:24, :] = row_ext[8:24, :] * left_inv[...]
     col_ext[8:136, :] = col_acc[...] * right_inv[...]
@@ -566,7 +626,6 @@
     @pl.when(col_lead & jnp.logical_not(col_lead_self))
     def _():
         wait_send(col_msg.at[pl.ds(0, 1)], 12)
-
 
 def body(
     pair_state,
@@ -581,8 +640,18 @@
     right_weight,
 ):
     vmem = pl.BlockSpec(memory_space=pltpu.VMEM)
+    hbm = pl.BlockSpec(memory_space=pl.ANY)
     rows = (ROWS, CH, COLS)
     scratch = [
+        (rows, BF16),
+        (rows, BF16),
+        ((DEV, CH), BF16),
+        ((1, DEV), jnp.int32),
+        ((CH, 5 * CH), BF16),
+        ((CH, CH), BF16),
+        ((CH, 3 * CH), BF16),
+        ((3 * CH, CH), BF16),
+        ((3 * CH, CH), BF16),
         ((8, DEV), F32),
         ((DEV, 3 * CH), F32),
         ((2, 8, CH), F32),
@@ -629,23 +698,12 @@
             jax.ShapeDtypeStruct(pair_state.shape, BF16),
             jax.ShapeDtypeStruct(atom_feats.shape, BF16),
         ),
-        in_specs=[
-            vmem,
-            vmem,
-            vmem,
-            vmem,
-            pl.BlockSpec(memory_space=pltpu.SMEM),
-            vmem,
-            vmem,
-            vmem,
-            vmem,
-            vmem,
-        ],
+        in_specs=[hbm] * 4 + [pl.BlockSpec(memory_space=pltpu.SMEM)] + [hbm] * 5,
         out_specs=(vmem, vmem),
         scratch_shapes=[pltpu.VMEM(shape, dtype) for shape, dtype in scratch]
-        + [pltpu.SemaphoreType.DMA((13,)), pltpu.SemaphoreType.DMA((13,))],
+        + [pltpu.SemaphoreType.DMA((n,)) for n in (13, 13, 9)],
         compiler_params=pltpu.CompilerParams(
-            has_side_effects=True, vmem_limit_bytes=48 * 2**20
+            collective_id=0, has_side_effects=True, vmem_limit_bytes=60 * 2**20
         ),
         cost_estimate=pl.CostEstimate(
             flops=1_700_000_000, bytes_accessed=2**21, transcendentals=2**20
@@ -662,7 +720,6 @@
         left_weight,
         right_weight,
     )
-
 
 def solution(mesh):
     placed = (

time: 114 us -> 93.7 us (0.82)
  Pallas kernels: 103 us -> 90.4 us
  local copies, waits for them, and re-layouts: 9.25 us -> 2.51 us
    pallas_call x1, Pallas kernels: 103 us -> 90.4 us  [body(): pl.pallas_call(kernel, out_shape=(jax.ShapeDtypeStruct(pair_state.shape,...]
    unnamed x22 -> x4, local copies, waits for them, and re-layouts: 9.25 us -> 2.51 us
where the time goes in v2:
time: 93.7 us; the launch traced here: 93.6 us
  Pallas kernels  90.4 us (96%)
  local copies, waits for them, and re-layouts  2.51 us (3%)
    pallas_call x1, Pallas kernels, body(): pl.pallas_call(kernel, out_shape=(jax.ShapeDtypeStruct(pair_state.shape,...  90.4 us
    unnamed x4, local copies, waits for them, and re-layouts  2.51 us

profile of v2, /device:TPU:1, one launch (start us, length us, event | category | flops | bytes accessed | tf_op | source)
XLA Modules:
  0.0 93.6 jit_solution(18287753065844013873)
XLA Ops:
  0.6 90.4 %shard_map.113 = (bf16[16,128,128]{2,1,0:T(8,128)(2,1)}, bf16[128,128]{1,0:T(8,128)(2,1)}) custom-call(bf16[16,128,128]{2,1,0:T(8,128)(2,1)} %pair_hbm.1, bf16[16,128,128]{2,1,0:T(8,128)(2,1)} %cot_hbm.1, bf16[128,128]{1,0:T(8,128)(2,1)} %feat_hbm.1, s32[1,128]{1,0:T(1,128)} %bitcast.1, s32[4]{0:T(128)} %count_ref.1, bf16[128,640]{1,0:T(8,128)(2,1)} %iw_hbm.1, ...), custom_call_target="tpu_custom_call" | custom-call | flops 1700000000 | bytes 2097152 | tf_op jit(solution)/shard_map/pallas_call | solution.py:695
  91.0 0.0 copy-start
  91.1 1.9 %copy.14 = bf16[16,128,128]{2,1,0:T(8,128)(2,1)} copy(bf16[16,128,128]{2,1,0:T(8,128)(2,1)} %get-tuple-element.4) | data formatting | bytes 1048576
  92.9 0.0 copy-done
  92.9 0.6 copy.15
Async XLA Ops:
  91.0 1.9 %copy-start = (bf16[128,128]{1,0:T(8,128)(2,1)S(1)}, bf16[128,128]{1,0:T(8,128)(2,1)}, u32[]{:S(2)}) copy-start(bf16[128,128]{1,0:T(8,128)(2,1)} %get-tuple-element.5) | copy-start | bytes 98308

commit v3 on v2

--- a/solution.py
+++ b/solution.py
@@ -17,23 +17,31 @@
 PAIR_DEV = 32
 ATOM_DEV = 4
 CHUNK = 32
-UNROLL = 4
+UNROLL = 16
+BIAS_ROWS = 6
+SUM_ROWS = 5
+
 
 def dot_nn(a, b):
     return lax.dot_general(a, b, (((1,), (0,)), ((), ())), preferred_element_type=F32)
 
+
 def dot_nt(a, b):
     return lax.dot_general(a, b, (((1,), (1,)), ((), ())), preferred_element_type=F32)
 
+
 def dot_tn(a, b):
     return lax.dot_general(a, b, (((0,), (0,)), ((), ())), preferred_element_type=F32)
+
 
 def split(x):
     high = x.astype(BF16)
     return high, (x - high.astype(F32)).astype(BF16)
 
+
 def sigmoid(x):
     return 0.5 * jnp.tanh(0.5 * x) + 0.5
+
 
 def loop(start, stop, step, unroll=1):
     def run(i, carry):
@@ -41,6 +49,7 @@
         return carry
 
     lax.fori_loop(start, stop, run, 0, unroll=unroll)
+
 
 def kernel(
     pair_hbm,
@@ -53,7 +62,7 @@
     aw_hbm,
     lw_hbm,
     rw_hbm,
-    pg_ref,
+    pg_hbm,
     ag_ref,
     pair_ref,
     cot_ref,
@@ -96,6 +105,7 @@
     gp_in,
     grad_out,
     grad_in,
+    pg_ref,
     col_acc,
     row_ext,
     col_ext,
@@ -143,38 +153,28 @@
         pltpu.make_async_copy(ref, ref, send_sem.at[sem]).wait()
 
     def channel(p, a):
-        return ((p // 8 + (p // 2) % 4 + a) % 4) * CHUNK + ((p // 2) % 4) * 8 + a * 2 + p % 2
+        return ((p // 8 + (p // 2) % 4) % 4) * CHUNK + ((p // 2) % 4) * 8 + a * 2 + p % 2
 
     mine = channel(pos, y)
-    group = (z + x + y) % 4
+    group = (z + x) % 4
 
     def send_group(step, send_one, self_one):
         def one(q):
             xs = (x + q // 8) % 4
-            a = (y + (q // 2) % 4) % 4
-            p = ((group + step - xs - a + 8) % 4) * 8 + xs * 2 + (c + q % 2) % 2
-            send_one(p, a)
-
-        if step == 0:
+            p = ((group + step + 4 - xs) % 4) * 8 + xs * 2 + (c + q % 2) % 2
+            send_one(p, (y + (q // 2) % 4) % 4)
+
+        if step % 4 == 0:
             self_one()
             loop(1, CHUNK, one)
         else:
             loop(0, CHUNK, one)
 
-    def plane(step):
-        return (z + step) % 4
-
-    def send_plane(step, zc, send_one, self_one):
-        def one(q):
-            p = zc * 8 + ((x + q // 8) % 4) * 2 + (c + q % 2) % 2
-            a = (y + (q // 2) % 4) % 4
-            send_one(p, a)
-
-        if step == 0:
-            self_one()
-            loop(1, CHUNK, one)
-        else:
-            loop(0, CHUNK, one)
+    def group_rows(zc):
+        return [
+            pl.ds(pl.multiple_of((((zc + 4 - xs) % 4) * 8 + xs * 2) * ROWS, 2 * ROWS), 2 * ROWS)
+            for xs in range(4)
+        ]
 
     barrier = pltpu.get_barrier_semaphore()
 
@@ -238,16 +238,20 @@
     for q in range(4):
         turned = iw_ref[:, q * CH : (q + 1) * CH].astype(F32).T.astype(BF16)
         for zc in range(4):
-            wt_ref[zc, q * CHUNK : (q + 1) * CHUNK, :] = turned[zc * CHUNK : (zc + 1) * CHUNK, :]
+            part = turned[zc * CHUNK : (zc + 1) * CHUNK, :]
+            at = slice((q % 2) * CHUNK, (q % 2 + 1) * CHUNK)
+            wt_ref[q // 2, zc, 0, at, :] = part
+            wt_ref[q // 2, (zc + 3) % 4, 1, at, :] = part
     wt5_ref[...] = iw_ref[:, 4 * CH :].astype(F32).T.astype(BF16)
     mt_ref[...] = ow_ref[...].astype(F32).T.astype(BF16)
 
+
     pl.semaphore_wait(barrier, DEV - 1)
 
     block = me // PAIR_DEV
     place = me % PAIR_DEV
-    right_src = bias_msg.at[1]
-    right_dst = right_in.at[pl.ds(pl.multiple_of(place * 8, 8), 8)]
+    right_src = bias_msg.at[1, pl.ds(0, BIAS_ROWS)]
+    right_dst = right_in.at[pl.ds(pl.multiple_of(place * 8, 8), BIAS_ROWS)]
     right_self = block == y
     either(right_src, right_dst, 0, pos, block, right_self)
     loop(1, PAIR_DEV, lambda q: remote(right_src, right_dst, 0, (pos + q) % PAIR_DEV, block))
@@ -256,14 +260,14 @@
 
     @pl.when(right_lead)
     def _():
-        lead_dst = right_in.at[pl.ds(PAIR_DEV * 8, 8)]
+        lead_dst = right_in.at[pl.ds(PAIR_DEV * 8, BIAS_ROWS)]
         either(right_src, lead_dst, 1, pos, block - 1, block - 1 == y)
         loop(
             1, PAIR_DEV, lambda q: remote(right_src, lead_dst, 1, (pos + q) % PAIR_DEV, block - 1)
         )
 
-    left_src = bias_msg.at[0]
-    left_dst = left_in.at[pl.ds(pl.multiple_of(y * 8, 8), 8)]
+    left_src = bias_msg.at[0, pl.ds(0, BIAS_ROWS)]
+    left_dst = left_in.at[pl.ds(pl.multiple_of(y * 8, 8), BIAS_ROWS)]
     local(left_src, left_dst, 2)
     loop(1, ATOM_DEV, lambda q: remote(left_src, left_dst, 2, pos, (y + q) % ATOM_DEV))
     left_lead = (y == 0) & (pos > 0)
@@ -274,7 +278,11 @@
             0,
             ATOM_DEV,
             lambda q: remote(
-                left_src, left_in.at[pl.ds(ATOM_DEV * 8, 8)], 3, pos - 1, (y + q) % ATOM_DEV
+                left_src,
+                left_in.at[pl.ds(ATOM_DEV * 8, BIAS_ROWS)],
+                3,
+                pos - 1,
+                (y + q) % ATOM_DEV,
             ),
         )
 
@@ -286,17 +294,18 @@
     def _():
         left_in[pl.ds(ATOM_DEV * 8, 8), :] = jnp.zeros((8, CH), F32)
 
-    wait_recv(right_in.at[pl.ds(0, PAIR_DEV * 8)], 0)
+    wait_recv(right_in.at[pl.ds(0, PAIR_DEV * BIAS_ROWS)], 0)
 
     @pl.when(y < ATOM_DEV - 1)
     def _():
-        wait_recv(right_in.at[pl.ds(PAIR_DEV * 8, 8)], 1)
-
-    wait_recv(left_in.at[pl.ds(0, ATOM_DEV * 8)], 2)
+        wait_recv(right_in.at[pl.ds(PAIR_DEV * 8, BIAS_ROWS)], 1)
+
+    wait_recv(left_in.at[pl.ds(0, ATOM_DEV * BIAS_ROWS)], 2)
 
     @pl.when(pos < PAIR_DEV - 1)
     def _():
-        wait_recv(left_in.at[pl.ds(ATOM_DEV * 8, 8)], 3)
+        wait_recv(left_in.at[pl.ds(ATOM_DEV * 8, BIAS_ROWS)], 3)
+
 
     def finish_bias(src, bias_ref, inverse_ref, n):
         lane = lax.broadcasted_iota(jnp.int32, (n, CH), 1)
@@ -315,6 +324,7 @@
     finish_bias(right_in, right_bias, right_inv, PAIR_DEV)
     finish_bias(left_in, left_bias, left_inv, ATOM_DEV)
 
+
     def front(r):
         values = pair_ref[r].astype(F32) + left_bias[pl.ds(r, 1), :] + right_bias[...]
         values = values.T
@@ -328,37 +338,42 @@
 
     loop(0, ROWS, front, UNROLL)
 
-    edge_dst = edge_in.at[:, y, pl.ds(pl.multiple_of(pos * ROWS, ROWS), ROWS)]
-    for step in range(4):
-        zc = (group + step) % 4
-        first = pl.multiple_of(zc * CHUNK, CHUNK)
-
-        def edges(r):
-            pre = dot_nn(wt_ref[zc], hidden_ref[r])
-            left_sig = sigmoid(pre[CHUNK : 2 * CHUNK])
-            right_sig = sigmoid(pre[3 * CHUNK :])
-            left = left_sig * pre[:CHUNK]
-            right = right_sig * pre[2 * CHUNK : 3 * CHUNK]
-            work_a[pl.ds(r, CHUNK, stride=ROWS), :] = left
-            work_b[pl.ds(r, CHUNK, stride=ROWS), :] = right
-            sig_left[r, pl.ds(first, CHUNK), :] = left_sig
-            sig_right[r, pl.ds(first, CHUNK), :] = right_sig
-            der_left[r, pl.ds(first, CHUNK), :] = left * (1.0 - left_sig)
-            der_right[r, pl.ds(first, CHUNK), :] = right * (1.0 - right_sig)
-
-        loop(0, ROWS, edges, UNROLL)
-        span = CHUNK * ROWS
-        edge_out[0, pl.ds(first, CHUNK)] = (
-            work_a[:span, :].reshape(CHUNK, ROWS, COLS).astype(BF16)
-        )
-        edge_out[1, pl.ds(first, CHUNK)] = (
-            work_b[:span, :].reshape(CHUNK, ROWS, COLS).astype(BF16)
-        )
-        send_group(
-            step,
-            lambda p, a: remote(edge_out.at[:, channel(p, a)], edge_dst, 4, p, a),
-            lambda: local(edge_out.at[:, mine], edge_dst, 4),
-        )
+
+    rows_here = pl.ds(pl.multiple_of(pos * ROWS, ROWS), ROWS)
+    for side, sig_ref, der_ref, work in (
+        (1, sig_right, der_right, work_b),
+        (0, sig_left, der_left, work_a),
+    ):
+        edge_dst = edge_in.at[side, y, rows_here]
+        for half in range(2):
+            groups = [(group + 2 * half + n) % 4 for n in range(2)]
+            firsts = [pl.multiple_of(zc * CHUNK, CHUNK) for zc in groups]
+
+            def edges(r):
+                weight = wt_ref[side, groups[0]].reshape(4 * CHUNK, CH)
+                pre = dot_nn(weight, hidden_ref[r])
+                for n in range(2):
+                    value = pre[2 * n * CHUNK : (2 * n + 1) * CHUNK]
+                    opened = sigmoid(pre[(2 * n + 1) * CHUNK : (2 * n + 2) * CHUNK])
+                    edge = opened * value
+                    work[pl.ds(n * CHUNK * ROWS + r, CHUNK, stride=ROWS), :] = edge
+                    sig_ref[r, pl.ds(firsts[n], CHUNK), :] = opened
+                    der_ref[r, pl.ds(firsts[n], CHUNK), :] = edge * (1.0 - opened)
+
+            loop(0, ROWS, edges, UNROLL)
+            for n in range(2):
+                edge_out[side, pl.ds(firsts[n], CHUNK)] = (
+                    work[n * CHUNK * ROWS : (n + 1) * CHUNK * ROWS, :]
+                    .reshape(CHUNK, ROWS, COLS)
+                    .astype(BF16)
+                )
+                step = 2 * half + n
+                sem = 4 if side == 1 else 13 + step
+                send_group(
+                    step,
+                    lambda p, a: remote(edge_out.at[side, channel(p, a)], edge_dst, sem, p, a),
+                    lambda: local(edge_out.at[side, mine], edge_dst, sem),
+                )
 
     def gate(r):
         opened = sigmoid(dot_nn(wt5_ref[...], hidden_ref[r]))
@@ -375,28 +390,32 @@
     zero = jnp.zeros((ROWS, COLS), F32)
     gn_mean = lax.fori_loop(0, 16, total, zero) * (1.0 / CH)
 
-    wait_recv(edge_in, 4)
 
     prod_dst = prod_in.at[mine]
+
+    def block_of(ref, p, a):
+        return ref.at[a, pl.ds(pl.multiple_of(p * ROWS, ROWS), ROWS)]
+
+    wait_recv(edge_in.at[1], 4)
     for step in range(4):
-        zc = plane(step)
-        first = pl.multiple_of(zc * 128, 128)
-        product = dot_nt(edge_in[0, 0, pl.ds(first, 128), :], edge_in[1, 0])
-        for a in range(1, 4):
-            product = product + dot_nt(edge_in[0, a, pl.ds(first, 128), :], edge_in[1, a])
+        wait_recv(edge_in.at[0, 0], 13 + step)
+        rows = group_rows((group + 4 - step) % 4)
+        product = None
         for a in range(4):
-            prod_out[a, pl.ds(first, 128), :] = product[:, a * 128 : (a + 1) * 128].astype(BF16)
-
-        def block_of(ref, p, a):
-            return ref.at[a, pl.ds(pl.multiple_of(p * ROWS, ROWS), ROWS)]
-
-        send_plane(
-            step,
-            zc,
+            lhs = jnp.concatenate([edge_in[0, a, run, :] for run in rows], axis=0)
+            term = dot_nt(lhs, edge_in[1, a])
+            product = term if product is None else product + term
+        product = product.astype(BF16)
+        for a in range(4):
+            for n, run in enumerate(rows):
+                prod_out[a, run, :] = product[
+                    2 * ROWS * n : 2 * ROWS * (n + 1), COLS * a : COLS * (a + 1)
+                ]
+        send_group(
+            (4 - step) % 4,
             lambda p, a: remote(block_of(prod_out, p, a), prod_dst, 5, p, a),
             lambda: local(block_of(prod_out, pos, y), prod_dst, 5),
         )
-
     wait_recv(prod_in, 5)
 
     def sum_prod(i, acc):
@@ -417,7 +436,8 @@
     prod_inv = lax.rsqrt(squares * (1.0 / CH) + EPSILON)
     cross = cross * prod_inv * prod_inv * (1.0 / CH)
 
-    gp_dst = gp_in.at[y, pl.ds(pl.multiple_of(pos * ROWS, ROWS), ROWS)]
+
+    gp_dst = gp_in.at[y, rows_here]
     for step in range(4):
         zc = (group + step) % 4
 
@@ -429,18 +449,47 @@
             grad = prod_inv[None] * (upstream - gn_mean[None] - shifted * cross[None])
             gp_out[pl.ds(at, 8)] = grad.astype(BF16)
 
-        loop(0, 4, grads)
+        loop(0, 4, grads, 4)
         send_group(
             step,
-            lambda p, a: remote(gp_out.at[channel(p, a)], gp_dst, 6, p, a),
-            lambda: local(gp_out.at[mine], gp_dst, 6),
+            lambda p, a: remote(gp_out.at[channel(p, a)], gp_dst, 17 + step, p, a),
+            lambda: local(gp_out.at[mine], gp_dst, 17 + step),
+        )
+
+
+    left_dst = grad_in.at[0, mine]
+    for step in range(4):
+        wait_recv(gp_in.at[0], 17 + step)
+        rows = group_rows((group + 4 - step) % 4)
+        lhs = jnp.concatenate(
+            [jnp.concatenate([gp_in[a, run, :] for run in rows], axis=0) for a in range(4)], axis=1
+        )
+        for a in range(4):
+            grad = dot_nn(lhs, edge_in[1, a]).astype(BF16)
+            for n, run in enumerate(rows):
+                grad_out[0, a, run, :] = grad[2 * ROWS * n : 2 * ROWS * (n + 1), :]
+        send_group(
+            (4 - step) % 4,
+            lambda p, a: remote(block_of(grad_out.at[0], p, a), left_dst, 7, p, a),
+            lambda: local(block_of(grad_out.at[0], pos, y), left_dst, 7),
+        )
+    for zc in range(4):
+        lhs = gp_in[zc].T
+        for a in range(4):
+            grad_out[1, a, 128 * zc : 128 * (zc + 1), :] = dot_nn(lhs, edge_in[0, a]).astype(BF16)
+    right_dst = grad_in.at[1, mine]
+    for step in range(4):
+        send_group(
+            step,
+            lambda p, a: remote(block_of(grad_out.at[1], p, a), right_dst, 8, p, a),
+            lambda: local(block_of(grad_out.at[1], pos, y), right_dst, 8),
         )
 
     def lay_normed(i):
         shifted = (prod_in[pl.ds(i * 8, 8)].astype(F32) - prod_mean[None]) * prod_inv[None]
         work_a[pl.ds(pl.multiple_of(i * 128, 128), 128), :] = shifted.reshape(128, COLS)
 
-    loop(0, 16, lay_normed)
+    loop(0, 16, lay_normed, UNROLL)
 
     def gate_grad(r):
         normed = work_a[pl.ds(r, CH, stride=ROWS), :].astype(BF16)
@@ -448,60 +497,38 @@
 
     loop(0, ROWS, gate_grad, UNROLL)
 
-    wait_recv(gp_in, 6)
-
-    for side in range(2):
-        grad_dst = grad_in.at[side, mine]
-        for step in range(4):
-            zc = plane(step)
-            first = pl.multiple_of(zc * 128, 128)
-            if side == 0:
-                lhs = jnp.concatenate([gp_in[a, pl.ds(first, 128), :] for a in range(4)], axis=1)
-            else:
-                lhs = gp_in[zc].T
-            for a in range(4):
-                grad_out[side, a, pl.ds(first, 128), :] = dot_nn(
-                    lhs, edge_in[1 - side, a]
-                ).astype(BF16)
-
-            def grad_block(p, a):
-                return grad_out.at[side, a, pl.ds(pl.multiple_of(p * ROWS, ROWS), ROWS)]
-
-            send_plane(
-                step,
-                zc,
-                lambda p, a: remote(grad_block(p, a), grad_dst, 7 + side, p, a),
-                lambda: local(grad_block(pos, y), grad_dst, 7 + side),
-            )
 
     row_ext[...] = jnp.zeros_like(row_ext)
     col_ext[...] = jnp.zeros_like(col_ext)
     col_acc[...] = jnp.zeros_like(col_acc)
 
-    for side, work in ((0, work_a), (1, work_b)):
-        wait_recv(grad_in.at[side], 7 + side)
-
-        def lay_grads(i):
+    def lay_grads(side, work):
+        def lay(i):
             work[pl.ds(pl.multiple_of(i * 128, 128), 128), :] = (
                 grad_in[side, pl.ds(i * 8, 8)].astype(F32).reshape(128, COLS)
             )
 
-        loop(0, 16, lay_grads)
+        loop(0, 16, lay, UNROLL)
+
+    def branches(work, sig_ref, der_ref, r):
+        flow = work[pl.ds(r, CH, stride=ROWS), :]
+        return [(flow * sig_ref[r]).astype(BF16), (flow * der_ref[r]).astype(BF16)]
+
+    def partial(r):
+        left = branches(work_a, sig_left, der_left, r)
+        gate_ref[r] = dot_nn(iw_ref[:, : 2 * CH], jnp.concatenate(left, axis=0)) + dot_nn(
+            iw_ref[:, 4 * CH :], gg_ref[r]
+        )
+
+    wait_recv(grad_in.at[0], 7)
+    lay_grads(0, work_a)
+    loop(0, ROWS, partial, UNROLL)
+    wait_recv(grad_in.at[1], 8)
+    lay_grads(1, work_b)
 
     def last(r):
-        left = work_a[pl.ds(r, CH, stride=ROWS), :]
-        right = work_b[pl.ds(r, CH, stride=ROWS), :]
-        branches = jnp.concatenate(
-            [
-                (left * sig_left[r]).astype(BF16),
-                (left * der_left[r]).astype(BF16),
-                (right * sig_right[r]).astype(BF16),
-                (right * der_right[r]).astype(BF16),
-                gg_ref[r],
-            ],
-            axis=0,
-        )
-        grad = dot_nn(iw_ref[...], branches)
+        right = branches(work_b, sig_right, der_right, r)
+        grad = gate_ref[r] + dot_nn(iw_ref[:, 2 * CH : 4 * CH], jnp.concatenate(right, axis=0))
         normed = normed_ref[r]
         first_mean = jnp.mean(grad, axis=0, keepdims=True)
         cross_mean = jnp.mean(grad * normed, axis=0, keepdims=True)
@@ -513,6 +540,10 @@
 
     loop(0, ROWS, last, UNROLL)
 
+
+    store = pltpu.make_async_copy(pg_ref, pg_hbm, load_sem.at[9])
+    store.start()
+
     row_ext[8:24, :] = row_ext[8:24, :] * left_inv[...]
     col_ext[8:136, :] = col_acc[...] * right_inv[...]
     for m in range(ATOM_DEV + 1):
@@ -520,24 +551,25 @@
     for m in range(PAIR_DEV + 1):
         col_msg[m] = col_ext[7 + 4 * m : 15 + 4 * m, :]
 
-    local(row_msg.at[y], row_in.at[y], 9)
+    used = pl.ds(0, SUM_ROWS)
+    local(row_msg.at[y, used], row_in.at[y, used], 9)
 
     def send_row(q):
         a = (y + q) % ATOM_DEV
-        remote(row_msg.at[a], row_in.at[y], 9, pos, a)
+        remote(row_msg.at[a, used], row_in.at[y, used], 9, pos, a)
 
     loop(1, ATOM_DEV, send_row)
     row_lead = pos < PAIR_DEV - 1
 
     @pl.when(row_lead)
     def _():
-        remote(row_msg.at[ATOM_DEV], row_in.at[ATOM_DEV + y], 10, pos + 1, 0)
+        remote(row_msg.at[ATOM_DEV, used], row_in.at[ATOM_DEV + y, used], 10, pos + 1, 0)
 
     def send_col(q):
         m = (place + q) % PAIR_DEV
         p = y * 8 + m // 4
         a = m % 4
-        either(col_msg.at[m], col_in.at[pos], 11, p, a, (p == pos) & (a == y))
+        either(col_msg.at[m, used], col_in.at[pos, used], 11, p, a, (p == pos) & (a == y))
 
     loop(0, PAIR_DEV, send_col)
     col_lead = y < ATOM_DEV - 1
@@ -546,8 +578,8 @@
     @pl.when(col_lead)
     def _():
         either(
-            col_msg.at[PAIR_DEV],
-            col_in.at[PAIR_DEV + pos],
+            col_msg.at[PAIR_DEV, used],
+            col_in.at[PAIR_DEV + pos, used],
             12,
             (y + 1) * 8,
             0,
@@ -565,67 +597,75 @@
     def _():
         col_in[PAIR_DEV:] = jnp.zeros((PAIR_DEV, 8, CH), F32)
 
-    wait_recv(row_in.at[pl.ds(0, ATOM_DEV)], 9)
+    wait_recv(row_in.at[pl.ds(0, ATOM_DEV), used], 9)
 
     @pl.when(row_more)
     def _():
-        wait_recv(row_in.at[pl.ds(ATOM_DEV, ATOM_DEV)], 10)
-
-    wait_recv(col_in.at[pl.ds(0, PAIR_DEV)], 11)
+        wait_recv(row_in.at[pl.ds(ATOM_DEV, ATOM_DEV), used], 10)
+
+    wait_recv(col_in.at[pl.ds(0, PAIR_DEV), used], 11)
 
     @pl.when(col_more)
     def _():
-        wait_recv(col_in.at[pl.ds(PAIR_DEV, PAIR_DEV)], 12)
+        wait_recv(col_in.at[pl.ds(PAIR_DEV, PAIR_DEV), used], 12)
+
 
     single = jnp.zeros((8, 3 * CH), F32)
     for ref, w_ref in ((row_in, lw_ref), (col_in, rw_ref)):
         weight = w_ref[...]
-        for part in split(jnp.sum(ref[...], axis=0)):
+        sums = jnp.where(row8 < SUM_ROWS, jnp.sum(ref[...], axis=0), 0.0)
+        for part in split(sums):
             single = single + dot_nt(part, weight)
     picked = dot_tn(member_ref[...].astype(BF16), single.astype(BF16))
     atom_grad = (picked * dsilu_ref[...]).astype(BF16)
     ag_ref[...] = dot_nt(atom_grad, aw_ref[...]).astype(BF16)
 
-    wait_send(right_in.at[pl.ds(0, (PAIR_DEV - 1) * 8)], 0)
+    store.wait()
+
+    wait_send(right_in.at[pl.ds(0, (PAIR_DEV - 1) * BIAS_ROWS)], 0)
 
     @pl.when(jnp.logical_not(right_self))
     def _():
-        wait_send(right_in.at[pl.ds(0, 8)], 0)
+        wait_send(right_in.at[pl.ds(0, BIAS_ROWS)], 0)
 
     @pl.when(right_lead)
     def _():
-        wait_send(right_in.at[pl.ds(0, (PAIR_DEV - 1) * 8)], 1)
+        wait_send(right_in.at[pl.ds(0, (PAIR_DEV - 1) * BIAS_ROWS)], 1)
 
         @pl.when(jnp.logical_not(right_lead_self))
         def _():
-            wait_send(right_in.at[pl.ds(0, 8)], 1)
-
-    wait_send(left_in.at[pl.ds(0, (ATOM_DEV - 1) * 8)], 2)
+            wait_send(right_in.at[pl.ds(0, BIAS_ROWS)], 1)
+
+    wait_send(left_in.at[pl.ds(0, (ATOM_DEV - 1) * BIAS_ROWS)], 2)
 
     @pl.when(left_lead)
     def _():
-        wait_send(left_in.at[pl.ds(0, ATOM_DEV * 8)], 3)
-
-    wait_send(edge_out.at[:, pl.ds(0, DEV - 1)], 4)
+        wait_send(left_in.at[pl.ds(0, ATOM_DEV * BIAS_ROWS)], 3)
+
+    wait_send(edge_out.at[1, pl.ds(0, DEV - 1)], 4)
+    for step in range(4):
+        sent = pl.ds(0, CHUNK - 1 if step == 0 else CHUNK)
+        wait_send(edge_out.at[0, sent], 13 + step)
+        wait_send(gp_out.at[sent], 17 + step)
     wait_send(prod_in.at[pl.ds(0, DEV - 1)], 5)
-    wait_send(gp_out.at[pl.ds(0, DEV - 1)], 6)
     for side in range(2):
         wait_send(grad_in.at[side, pl.ds(0, DEV - 1)], 7 + side)
-    wait_send(row_msg.at[pl.ds(0, ATOM_DEV - 1)], 9)
+    wait_send(row_msg.at[pl.ds(0, ATOM_DEV - 1), used], 9)
 
     @pl.when(row_lead)
     def _():
-        wait_send(row_msg.at[pl.ds(0, 1)], 10)
-
-    wait_send(col_msg.at[pl.ds(0, PAIR_DEV - 1)], 11)
+        wait_send(row_msg.at[pl.ds(0, 1), used], 10)
+
+    wait_send(col_msg.at[pl.ds(0, PAIR_DEV - 1), used], 11)
 
     @pl.when(block != y)
     def _():
-        wait_send(col_msg.at[pl.ds(0, 1)], 11)
+        wait_send(col_msg.at[pl.ds(0, 1), used], 11)
 
     @pl.when(col_lead & jnp.logical_not(col_lead_self))
     def _():
-        wait_send(col_msg.at[pl.ds(0, 1)], 12)
+        wait_send(col_msg.at[pl.ds(0, 1), used], 12)
+
 
 def body(
     pair_state,
@@ -661,7 +701,7 @@
         ((COLS, CH), F32),
         ((ROWS, CH), F32),
         ((ROWS, CH), F32),
-        ((4, 4 * CHUNK, CH), BF16),
+        ((2, 4, 2, 2 * CHUNK, CH), BF16),
         ((CH, CH), BF16),
         ((CH, CH), BF16),
         (rows, F32),
@@ -684,6 +724,7 @@
         ((4, TOK, COLS), BF16),
         ((2, 4, TOK, COLS), BF16),
         ((2, DEV, ROWS, COLS), BF16),
+        (rows, BF16),
         ((COLS, CH), F32),
         ((40, CH), F32),
         ((152, CH), F32),
@@ -699,9 +740,9 @@
             jax.ShapeDtypeStruct(atom_feats.shape, BF16),
         ),
         in_specs=[hbm] * 4 + [pl.BlockSpec(memory_space=pltpu.SMEM)] + [hbm] * 5,
-        out_specs=(vmem, vmem),
+        out_specs=(hbm, vmem),
         scratch_shapes=[pltpu.VMEM(shape, dtype) for shape, dtype in scratch]
-        + [pltpu.SemaphoreType.DMA((n,)) for n in (13, 13, 9)],
+        + [pltpu.SemaphoreType.DMA((n,)) for n in (21, 21, 10)],
         compiler_params=pltpu.CompilerParams(
             collective_id=0, has_side_effects=True, vmem_limit_bytes=60 * 2**20
         ),
@@ -720,6 +761,7 @@
         left_weight,
         right_weight,
     )
+
 
 def solution(mesh):
     placed = (

time: 93.7 us -> 82 us (0.88)
  Pallas kernels: 90.4 us -> 78.7 us
    pallas_call x1, Pallas kernels: 90.4 us -> 78.7 us  [body(): pl.pallas_call(kernel, out_shape=(jax.ShapeDtypeStruct(pair_state.shape,...]
where the time goes in v3:
time: 82 us; the launch traced here: 81.8 us
  Pallas kernels  78.7 us (96%)
  local copies, waits for them, and re-layouts  2.51 us (3%)
    pallas_call x1, Pallas kernels, body(): pl.pallas_call(kernel, out_shape=(jax.ShapeDtypeStruct(pair_state.shape,...  78.7 us
    unnamed x4, local copies, waits for them, and re-layouts  2.51 us

profile of v3, /device:TPU:1, one launch (start us, length us, event | category | flops | bytes accessed | tf_op | source)
XLA Modules:
  0.0 81.8 jit_solution(5967962482057743804)
XLA Ops:
  0.6 78.7 %shard_map.113 = (bf16[16,128,128]{2,1,0:T(8,128)(2,1)}, bf16[128,128]{1,0:T(8,128)(2,1)}) custom-call(bf16[16,128,128]{2,1,0:T(8,128)(2,1)} %pair_hbm.1, bf16[16,128,128]{2,1,0:T(8,128)(2,1)} %cot_hbm.1, bf16[128,128]{1,0:T(8,128)(2,1)} %feat_hbm.1, s32[1,128]{1,0:T(1,128)} %bitcast.1, s32[4]{0:T(128)} %count_ref.1, bf16[128,640]{1,0:T(8,128)(2,1)} %iw_hbm.1, ...), custom_call_target="tpu_custom_call" | custom-call | flops 1700000000 | bytes 2097152 | tf_op jit(solution)/shard_map/pallas_call | solution.py:736
  79.3 0.0 copy-start
  79.3 1.9 %copy.14 = bf16[16,128,128]{2,1,0:T(8,128)(2,1)} copy(bf16[16,128,128]{2,1,0:T(8,128)(2,1)} %get-tuple-element.4) | data formatting | bytes 1048576
  81.2 0.0 copy-done
  81.2 0.6 copy.15
Async XLA Ops:
  79.3 1.9 %copy-start = (bf16[128,128]{1,0:T(8,128)(2,1)S(1)}, bf16[128,128]{1,0:T(8,128)(2,1)}, u32[]{:S(2)}) copy-start(bf16[128,128]{1,0:T(8,128)(2,1)} %get-tuple-element.5) | copy-start | bytes 98308

commit v4 on v3

--- a/solution.py
+++ b/solution.py
@@ -160,9 +160,9 @@
 
     def send_group(step, send_one, self_one):
         def one(q):
-            xs = (x + q // 8) % 4
+            xs = (x + (q // 2) % 4) % 4
             p = ((group + step + 4 - xs) % 4) * 8 + xs * 2 + (c + q % 2) % 2
-            send_one(p, (y + (q // 2) % 4) % 4)
+            send_one(p, (y + q // 8) % 4)
 
         if step % 4 == 0:
             self_one()
@@ -175,19 +175,6 @@
             pl.ds(pl.multiple_of((((zc + 4 - xs) % 4) * 8 + xs * 2) * ROWS, 2 * ROWS), 2 * ROWS)
             for xs in range(4)
         ]
-
-    barrier = pltpu.get_barrier_semaphore()
-
-    def greet(q):
-        to = (me + q) % DEV
-        pl.semaphore_signal(
-            barrier,
-            inc=1,
-            device_id=(to // ATOM_DEV, to % ATOM_DEV),
-            device_id_type=pl.DeviceIdType.MESH,
-        )
-
-    loop(1, DEV, greet)
 
     loads = [
         pltpu.make_async_copy(src, dst, load_sem.at[n])
@@ -207,6 +194,45 @@
     ]
     for load in loads:
         load.start()
+    barrier = pltpu.get_barrier_semaphore()
+    block = me // PAIR_DEV
+    place = me % PAIR_DEV
+    lead_right = ((place == 0) & (me > 0)).astype(jnp.int32)
+    lead_left = ((y == 0) & (pos > 0)).astype(jnp.int32)
+
+    def greet(to):
+        @pl.when(to != me)
+        def _():
+            pl.semaphore_signal(
+                barrier,
+                inc=1,
+                device_id=(to // ATOM_DEV, to % ATOM_DEV),
+                device_id_type=pl.DeviceIdType.MESH,
+            )
+
+    loop(0, PAIR_DEV, lambda q: greet(y * PAIR_DEV + (place + q) % PAIR_DEV))
+    loop(1, ATOM_DEV, lambda q: greet(pos * ATOM_DEV + (y + q) % ATOM_DEV))
+    loop(0, ATOM_DEV, lambda q: greet(q * PAIR_DEV + pos))
+
+    @pl.when(y < ATOM_DEV - 1)
+    def _():
+        greet((y + 1) * PAIR_DEV)
+
+    @pl.when(pos < PAIR_DEV - 1)
+    def _():
+        greet((pos + 1) * ATOM_DEV)
+
+    greeted = (
+        PAIR_DEV
+        - (block == y).astype(jnp.int32)
+        + ATOM_DEV
+        - 1
+        + ATOM_DEV
+        - (place == pos).astype(jnp.int32)
+        + lead_right * (PAIR_DEV - (block == y + 1).astype(jnp.int32))
+        + lead_left * ATOM_DEV
+    )
+
     for load in loads[:5]:
         load.wait()
 
@@ -246,10 +272,8 @@
     mt_ref[...] = ow_ref[...].astype(F32).T.astype(BF16)
 
 
-    pl.semaphore_wait(barrier, DEV - 1)
-
-    block = me // PAIR_DEV
-    place = me % PAIR_DEV
+    pl.semaphore_wait(barrier, greeted)
+
     right_src = bias_msg.at[1, pl.ds(0, BIAS_ROWS)]
     right_dst = right_in.at[pl.ds(pl.multiple_of(place * 8, 8), BIAS_ROWS)]
     right_self = block == y

time: 82 us -> 78.6 us (0.959)
  Pallas kernels: 78.7 us -> 75.3 us
    pallas_call x1, Pallas kernels: 78.7 us -> 75.3 us  [body(): pl.pallas_call(kernel, out_shape=(jax.ShapeDtypeStruct(pair_state.shape,...]
where the time goes in v4:
time: 78.6 us; the launch traced here: 78.5 us
  Pallas kernels  75.3 us (96%)
  local copies, waits for them, and re-layouts  2.51 us (3%)
    pallas_call x1, Pallas kernels, body(): pl.pallas_call(kernel, out_shape=(jax.ShapeDtypeStruct(pair_state.shape,...  75.3 us
    unnamed x4, local copies, waits for them, and re-layouts  2.51 us

profile of v4, /device:TPU:1, one launch (start us, length us, event | category | flops | bytes accessed | tf_op | source)
XLA Modules:
  0.0 78.5 jit_solution(8773251944563754877)
XLA Ops:
  0.6 75.3 %shard_map.113 = (bf16[16,128,128]{2,1,0:T(8,128)(2,1)}, bf16[128,128]{1,0:T(8,128)(2,1)}) custom-call(bf16[16,128,128]{2,1,0:T(8,128)(2,1)} %pair_hbm.1, bf16[16,128,128]{2,1,0:T(8,128)(2,1)} %cot_hbm.1, bf16[128,128]{1,0:T(8,128)(2,1)} %feat_hbm.1, s32[1,128]{1,0:T(1,128)} %bitcast.1, s32[4]{0:T(128)} %count_ref.1, bf16[128,640]{1,0:T(8,128)(2,1)} %iw_hbm.1, ...), custom_call_target="tpu_custom_call" | custom-call | flops 1700000000 | bytes 2097152 | tf_op jit(solution)/shard_map/pallas_call | solution.py:760
  75.9 0.0 copy-start
  76.0 1.9 %copy.14 = bf16[16,128,128]{2,1,0:T(8,128)(2,1)} copy(bf16[16,128,128]{2,1,0:T(8,128)(2,1)} %get-tuple-element.4) | data formatting | bytes 1048576
  77.8 0.0 copy-done
  77.8 0.6 copy.15
Async XLA Ops:
  75.9 1.9 %copy-start = (bf16[128,128]{1,0:T(8,128)(2,1)S(1)}, bf16[128,128]{1,0:T(8,128)(2,1)}, u32[]{:S(2)}) copy-start(bf16[128,128]{1,0:T(8,128)(2,1)} %get-tuple-element.5) | copy-start | bytes 98308

commit v5 on v4

--- a/solution.py
+++ b/solution.py
@@ -20,6 +20,7 @@
 UNROLL = 16
 BIAS_ROWS = 6
 SUM_ROWS = 5
+PARTS = 4
 
 
 def dot_nn(a, b):
@@ -691,6 +692,28 @@
         wait_send(col_msg.at[pl.ds(0, 1), used], 12)
 
 
+def hand_over(pair_in, atom_in, pair_out, atom_out, pair_held, atom_held, in_sems, out_sems):
+    part = ROWS // PARTS
+    blocks = [
+        (pair_in.at[run], pair_held.at[run], pair_out.at[run])
+        for run in (pl.ds(n * part, part) for n in range(PARTS))
+    ]
+    blocks.append((atom_in, atom_held, atom_out))
+    loads = [
+        pltpu.make_async_copy(src, held, in_sems.at[n]) for n, (src, held, _) in enumerate(blocks)
+    ]
+    stores = [
+        pltpu.make_async_copy(held, dst, out_sems.at[n]) for n, (_, held, dst) in enumerate(blocks)
+    ]
+    for load in loads:
+        load.start()
+    for load, store in zip(loads, stores):
+        load.wait()
+        store.start()
+    for store in stores:
+        store.wait()
+
+
 def body(
     pair_state,
     cotangent,
@@ -757,7 +780,7 @@
         ((2 * ATOM_DEV, 8, CH), F32),
         ((2 * PAIR_DEV, 8, CH), F32),
     ]
-    return pl.pallas_call(
+    grads = pl.pallas_call(
         kernel,
         out_shape=(
             jax.ShapeDtypeStruct(pair_state.shape, BF16),
@@ -785,6 +808,19 @@
         left_weight,
         right_weight,
     )
+    return pl.pallas_call(
+        hand_over,
+        out_shape=tuple(jax.ShapeDtypeStruct(grad.shape, BF16) for grad in grads),
+        in_specs=[hbm, hbm],
+        out_specs=(hbm, hbm),
+        scratch_shapes=[
+            pltpu.VMEM((ROWS, COLS, CH), BF16),
+            pltpu.VMEM((DEV, CH), BF16),
+            pltpu.SemaphoreType.DMA((PARTS + 1,)),
+            pltpu.SemaphoreType.DMA((PARTS + 1,)),
+        ],
+        compiler_params=pltpu.CompilerParams(vmem_limit_bytes=60 * 2**20),
+    )(*grads)
 
 
 def solution(mesh):

time: 78.6 us -> 77.9 us (level)
  local copies, waits for them, and re-layouts: 2.51 us -> 0 us
  Pallas kernels: 75.3 us -> 77.1 us
    unnamed x4 -> x0, local copies, waits for them, and re-layouts: 2.51 us -> none
    pallas_call x0 -> x1, Pallas kernels: none -> 1.84 us  [body(): pl.pallas_call(hand_over, out_shape=tuple((jax.ShapeDtypeStruct(grad.shap...]
where the time goes in v5:
time: 77.9 us; the launch traced here: 77.8 us
  Pallas kernels  77.1 us (99%)
    pallas_call x1, Pallas kernels, body(): pl.pallas_call(kernel, out_shape=(jax.ShapeDtypeStruct(pair_state.shape,...  75.3 us
    pallas_call x1, Pallas kernels, body(): pl.pallas_call(hand_over, out_shape=tuple((jax.ShapeDtypeStruct(grad.shap...  1.84 us

profile of v5, /device:TPU:1, one launch (start us, length us, event | category | flops | bytes accessed | tf_op | source)
XLA Modules:
  0.0 77.8 jit_solution(9115093523370836533)
XLA Ops:
  0.6 75.3 %shard_map.113 = (bf16[16,128,128]{2,1,0:T(8,128)(2,1)}, bf16[128,128]{1,0:T(8,128)(2,1)}) custom-call(bf16[16,128,128]{2,1,0:T(8,128)(2,1)} %pair_hbm.1, bf16[16,128,128]{2,1,0:T(8,128)(2,1)} %cot_hbm.1, bf16[128,128]{1,0:T(8,128)(2,1)} %feat_hbm.1, s32[1,128]{1,0:T(1,128)} %bitcast.1, s32[4]{0:T(128)} %count_ref.1, bf16[128,640]{1,0:T(8,128)(2,1)} %iw_hbm.1, ...), custom_call_target="tpu_custom_call" | custom-call | flops 1700000000 | bytes 2097152 | tf_op jit(solution)/shard_map/pallas_call | solution.py:783
  75.9 1.8 %shard_map.114 = (bf16[16,128,128]{2,1,0:T(8,128)(2,1)}, bf16[128,128]{1,0:T(8,128)(2,1)}) custom-call(bf16[16,128,128]{2,1,0:T(8,128)(2,1)} %get-tuple-element.4.pair_in, bf16[128,128]{1,0:T(8,128)(2,1)} %get-tuple-element.5.atom_in), custom_call_target="tpu_custom_call" | custom-call | tf_op jit(solution)/shard_map/pallas_call | solution.py:811

commit v6 on v5

--- a/solution.py
+++ b/solution.py
@@ -260,6 +260,44 @@
         sums = dot_nn(high, weight) + dot_nn(low, weight)
         bias_msg[n] = jnp.where(row8 == 5, count_row, sums)
 
+    pl.semaphore_wait(barrier, greeted)
+
+    right_src = bias_msg.at[1, pl.ds(0, BIAS_ROWS)]
+    right_dst = right_in.at[pl.ds(pl.multiple_of(place * 8, 8), BIAS_ROWS)]
+    right_self = block == y
+    either(right_src, right_dst, 0, pos, block, right_self)
+    loop(1, PAIR_DEV, lambda q: remote(right_src, right_dst, 0, (pos + q) % PAIR_DEV, block))
+    right_lead = (place == 0) & (me > 0)
+    right_lead_self = right_lead & (block - 1 == y)
+
+    @pl.when(right_lead)
+    def _():
+        lead_dst = right_in.at[pl.ds(PAIR_DEV * 8, BIAS_ROWS)]
+        either(right_src, lead_dst, 1, pos, block - 1, block - 1 == y)
+        loop(
+            1, PAIR_DEV, lambda q: remote(right_src, lead_dst, 1, (pos + q) % PAIR_DEV, block - 1)
+        )
+
+    left_src = bias_msg.at[0, pl.ds(0, BIAS_ROWS)]
+    left_dst = left_in.at[pl.ds(pl.multiple_of(y * 8, 8), BIAS_ROWS)]
+    local(left_src, left_dst, 2)
+    loop(1, ATOM_DEV, lambda q: remote(left_src, left_dst, 2, pos, (y + q) % ATOM_DEV))
+    left_lead = (y == 0) & (pos > 0)
+
+    @pl.when(left_lead)
+    def _():
+        loop(
+            0,
+            ATOM_DEV,
+            lambda q: remote(
+                left_src,
+                left_in.at[pl.ds(ATOM_DEV * 8, BIAS_ROWS)],
+                3,
+                pos - 1,
+                (y + q) % ATOM_DEV,
+            ),
+        )
+
     for load in loads[5:]:
         load.wait()
     for q in range(4):
@@ -271,45 +309,6 @@
             wt_ref[q // 2, (zc + 3) % 4, 1, at, :] = part
     wt5_ref[...] = iw_ref[:, 4 * CH :].astype(F32).T.astype(BF16)
     mt_ref[...] = ow_ref[...].astype(F32).T.astype(BF16)
-
-
-    pl.semaphore_wait(barrier, greeted)
-
-    right_src = bias_msg.at[1, pl.ds(0, BIAS_ROWS)]
-    right_dst = right_in.at[pl.ds(pl.multiple_of(place * 8, 8), BIAS_ROWS)]
-    right_self = block == y
-    either(right_src, right_dst, 0, pos, block, right_self)
-    loop(1, PAIR_DEV, lambda q: remote(right_src, right_dst, 0, (pos + q) % PAIR_DEV, block))
-    right_lead = (place == 0) & (me > 0)
-    right_lead_self = right_lead & (block - 1 == y)
-
-    @pl.when(right_lead)
-    def _():
-        lead_dst = right_in.at[pl.ds(PAIR_DEV * 8, BIAS_ROWS)]
-        either(right_src, lead_dst, 1, pos, block - 1, block - 1 == y)
-        loop(
-            1, PAIR_DEV, lambda q: remote(right_src, lead_dst, 1, (pos + q) % PAIR_DEV, block - 1)
-        )
-
-    left_src = bias_msg.at[0, pl.ds(0, BIAS_ROWS)]
-    left_dst = left_in.at[pl.ds(pl.multiple_of(y * 8, 8), BIAS_ROWS)]
-    local(left_src, left_dst, 2)
-    loop(1, ATOM_DEV, lambda q: remote(left_src, left_dst, 2, pos, (y + q) % ATOM_DEV))
-    left_lead = (y == 0) & (pos > 0)
-
-    @pl.when(left_lead)
-    def _():
-        loop(
-            0,
-            ATOM_DEV,
-            lambda q: remote(
-                left_src,
-                left_in.at[pl.ds(ATOM_DEV * 8, BIAS_ROWS)],
-                3,
-                pos - 1,
-                (y + q) % ATOM_DEV,
-            ),
-        )
 
     @pl.when(y == ATOM_DEV - 1)
     def _():

time: 77.9 us -> 77.9 us (level)
  no operation moved by 1% of the time
where the time goes in v6:
time: 77.9 us; the launch traced here: 77.8 us
  Pallas kernels  77.1 us (99%)
    pallas_call x1, Pallas kernels, body(): pl.pallas_call(kernel, out_shape=(jax.ShapeDtypeStruct(pair_state.shape,...  75.3 us
    pallas_call x1, Pallas kernels, body(): pl.pallas_call(hand_over, out_shape=tuple((jax.ShapeDtypeStruct(grad.shap...  1.84 us

profile of v6, /device:TPU:1, one launch (start us, length us, event | category | flops | bytes accessed | tf_op | source)
XLA Modules:
  0.0 77.8 jit_solution(9119386037638643349)
XLA Ops:
  0.6 75.3 %shard_map.113 = (bf16[16,128,128]{2,1,0:T(8,128)(2,1)}, bf16[128,128]{1,0:T(8,128)(2,1)}) custom-call(bf16[16,128,128]{2,1,0:T(8,128)(2,1)} %pair_hbm.1, bf16[16,128,128]{2,1,0:T(8,128)(2,1)} %cot_hbm.1, bf16[128,128]{1,0:T(8,128)(2,1)} %feat_hbm.1, s32[1,128]{1,0:T(1,128)} %bitcast.1, s32[4]{0:T(128)} %count_ref.1, bf16[128,640]{1,0:T(8,128)(2,1)} %iw_hbm.1, ...), custom_call_target="tpu_custom_call" | custom-call | flops 1700000000 | bytes 2097152 | tf_op jit(solution)/shard_map/pallas_call | solution.py:782
  75.9 1.8 %shard_map.114 = (bf16[16,128,128]{2,1,0:T(8,128)(2,1)}, bf16[128,128]{1,0:T(8,128)(2,1)}) custom-call(bf16[16,128,128]{2,1,0:T(8,128)(2,1)} %get-tuple-element.4.pair_in, bf16[128,128]{1,0:T(8,128)(2,1)} %get-tuple-element.5.atom_in), custom_call_target="tpu_custom_call" | custom-call | tf_op jit(solution)/shard_map/pallas_call | solution.py:810
